TPU v7x, 256 devices: a whole 4x4x8 slice. The times are simulated.
256 devices in a mesh: section: 2 (over z_hi), dp: 8 (over x, core), tensor: 16 (over y, z_lo).
Axes of the slice: x: 4, y: 4, z: 8 (z_hi: 2, z_lo: 4; z = z_hi * 4 + z_lo), core: 2. Of those that a mesh axis runs over, the one named last changes fastest.
Arguments:
- hidden: bfloat16 [256, 16384], P('dp'), may hold values from -6 to 6
- query_weight: bfloat16 [2, 16384, 16384], P('section', 'dp', 'tensor'), may hold values from -0.046875 to 0.046875
- out_weight: bfloat16 [2, 16384, 16384], P('section', 'tensor', 'dp'), may hold values from -0.28125 to 0.28125
- key_cache: bfloat16 [2, 256, 256, 1024], P('section', 'dp', None, 'tensor'), may hold values from -400 to 400
- value_cache: bfloat16 [2, 256, 256, 1024], P('section', 'dp', None, 'tensor'), may hold values from -6 to 6
- cache_lengths: int32 [256], P('dp'), may hold values from 32 to 256, as said below
Outputs:
- layer_outputs: bfloat16 [2, 256, 16384], P('section', 'dp')
Inputs may be any that keep to these rules, and one draw needn't show every extreme that they name: `cache_lengths`: in every aligned block of 32 rows some row has all 256 positions live.
All inputs are finite; a program needn't handle non-finite values.
Results may differ from a plain program's by a relative error of at most 0.01595.
Values may be sent and summed in bfloat16 or wider, within the bound.
No kernel may reach another device: no remote copies, remote signals or barrier semaphores. Data moves between devices by JAX's collectives and lax.ppermute only.
A program may use at most 64 MiB of HBM per device.

v0:
```python
import functools

import jax
import jax.numpy as jnp
from jax import lax
from jax.experimental import pallas as pl
from jax.experimental.pallas import tpu as pltpu
from jax.sharding import Mesh, PartitionSpec as P

DP = ("x", "c")
DEPTH = ("zh", "zl")
TENSOR = ("y", "zh", "zl")
BF = jnp.bfloat16
F32 = jnp.float32
VMEM = pl.BlockSpec(memory_space=pltpu.VMEM)
SMEM = pl.BlockSpec(memory_space=pltpu.SMEM)
LIMIT = 16 * 1024 * 1024
GROUP = 16
Y, Z, HALF, SECTION, X, CORE = range(6)


def call(kernel, out_shapes, args, flops=0, scratch=(), name=None):
    single = not isinstance(out_shapes, (list, tuple))
    shapes = [out_shapes] if single else list(out_shapes)
    volume = sum(a.size * a.dtype.itemsize for a in list(args) + shapes)
    return pl.pallas_call(
        kernel,
        out_shape=out_shapes,
        in_specs=[
            SMEM if a.ndim == 1 else VMEM for a in args
        ],
        out_specs=VMEM if single else [VMEM] * len(shapes),
        scratch_shapes=list(scratch),
        compiler_params=pltpu.CompilerParams(vmem_limit_bytes=LIMIT),
        cost_estimate=pl.CostEstimate(flops=flops, bytes_accessed=volume, transcendentals=0),
        name=name,
    )(*args)


def moved(block, axes, step):
    if step == 0:
        return block
    pairs = [(i, i ^ step) for i in range(lax.axis_size(axes))]
    return lax.ppermute(block, axes, pairs)


def gathered(block, axes):
    return [moved(block, axes, step) for step in range(lax.axis_size(axes))]


def arrange(place_ref, hidden_ref, *out_refs):
    x, core = place_ref[X], place_ref[CORE]
    width = out_refs[0].shape[2]
    for step, out_ref in enumerate(out_refs):
        for side in range(2):
            part = (x ^ step) * 2 + (core ^ side)
            out_ref[side] = hidden_ref[:, pl.ds(pl.multiple_of(part * width, 128), width)]


def pick(*refs):
    out_ref = refs[-1]
    for step, ref in enumerate(refs[:-1]):
        out_ref[step] = ref[1] if len(ref.shape) == 3 else ref[...]


def project(held, weight_ref, near_ref, far_ref):
    rows = near_ref.shape[0]
    width = weight_ref.shape[1]
    for start, out_ref in ((rows, far_ref), (0, near_ref)):
        wide = held[start : start + rows].astype(F32)
        squares = jnp.sum(wide * wide, axis=1, keepdims=True)
        high = squares.astype(BF).astype(F32)
        middle = (squares - high).astype(BF).astype(F32)
        low = squares - high - middle
        lane = lax.broadcasted_iota(jnp.int32, (rows, 128), 1)
        pieces = jnp.where(lane == 0, high, jnp.where(lane == 1, middle, low))
        out_ref[:, width:] = jnp.where(lane < 3, pieces, 0.0).astype(BF)

    @pl.loop(0, width // 512)
    def _(tile):
        span = pl.ds(pl.multiple_of(tile * 512, 512), 512)
        product = jnp.dot(held[...], weight_ref[:, span], preferred_element_type=F32).astype(BF)
        near_ref[:, span] = product[:rows]
        far_ref[:, span] = product[rows:]


def project_rows(place_ref, a_ref, b_ref, c_ref, d_ref, other_ref, weight_ref, *refs):
    near_ref, far_ref, state_ref, held = refs
    rows = a_ref.shape[1]
    for step, ref in enumerate((a_ref, b_ref, c_ref, d_ref)):
        held[step * rows : (step + 1) * rows] = ref[0]
        held[(step + 4) * rows : (step + 5) * rows] = other_ref[step]
    start = (place_ref[Y] * 4 + place_ref[Z]) * 128
    state_ref[...] = held[:, pl.ds(pl.multiple_of(start, 128), 128)]
    project(held, weight_ref, near_ref, far_ref)


def project_columns(place_ref, a_ref, b_ref, c_ref, d_ref, weight_ref, near_ref, far_ref, held):
    y, z = place_ref[Y], place_ref[Z]
    for step, ref in enumerate((a_ref, b_ref, c_ref, d_ref)):
        for depth in range(4):
            index = (y ^ step) * 4 + (z ^ depth ^ 3)
            held[:, pl.ds(pl.multiple_of(index * 128, 128), 128)] = ref[depth]
    project(held, weight_ref, near_ref, far_ref)


def add_cores(near_ref, far_ref, *out_refs):
    rows = out_refs[0].shape[0]
    for step, out_ref in enumerate(out_refs):
        span = slice(step * rows, (step + 1) * rows)
        out_ref[...] = (near_ref[span].astype(F32) + far_ref[span].astype(F32)).astype(BF)


def queries_of(sums, width):
    total = sums[0][...].astype(F32)
    for block in sums[1:]:
        total += block[...].astype(F32)
    squares = total[:, width : width + 1] + total[:, width + 1 : width + 2]
    squares = squares + total[:, width + 2 : width + 3]
    return total[:, :width] * lax.rsqrt(squares / 16384.0 + 1e-05)


def group_attention(half, queries, heads, lengths_ref, start, caches):
    key, key_other, value, value_other = caches
    depth, cache_len = key.shape[1:]
    count = GROUP * heads
    lane = lax.broadcasted_iota(jnp.int32, (count, 128), 1)
    row = lax.rem(lax.broadcasted_iota(jnp.int32, (count, 128), 0), GROUP)
    first = lane < 64
    side = jnp.where(first, 0, 1)
    odd = lax.rem(row, 2)

    def diagonal(block):
        return jnp.concatenate(
            [jnp.where(row == 2 * k + side, block, 0.0).astype(BF) for k in range(GROUP // 2)],
            axis=1,
        )

    def blend(values):
        product = lax.dot_general(
            probs,
            values.reshape(GROUP * depth, cache_len),
            (((1,), (1,)), ((), ())),
            preferred_element_type=F32,
        )
        result = jnp.zeros((count, 128), F32)
        for k in range(GROUP // 2):
            result += jnp.where(row // 2 == k, product[:, k * 128 : (k + 1) * 128], 0.0)
        return result

    turned = pltpu.roll(queries, 64, 1)
    low = jnp.where(first, queries, turned)
    high = jnp.where(first, turned, queries)
    own_q = jnp.where(half == 0, low, high)
    other_q = jnp.where(half == 0, high, low)
    key = key.reshape(GROUP * depth, cache_len)
    key_other = key_other.reshape(GROUP * depth, cache_len)
    scores = jnp.dot(diagonal(own_q), key, preferred_element_type=F32)
    scores += jnp.dot(diagonal(other_q), key_other, preferred_element_type=F32)
    scores = scores * (128.0**-0.5)
    limits = jnp.zeros((count, 128), jnp.int32)
    for k in range(GROUP):
        limits = jnp.where(row == k, lengths_ref[start + k], limits)
    limits = jnp.concatenate([limits] * (cache_len // 128), axis=1)
    live = lax.broadcasted_iota(jnp.int32, scores.shape, 1) < limits
    scores = jnp.where(live, scores, -1e30)
    top = jnp.max(scores, axis=1, keepdims=True)
    expd = jnp.where(live, jnp.exp(scores - top), 0.0)
    probs = (expd / jnp.sum(expd, axis=1, keepdims=True)).astype(BF)
    own = blend(value)
    other = blend(value_other)
    own = jnp.where(odd == half, own, pltpu.roll(own, 64, 1))
    other = jnp.where(odd == half, pltpu.roll(other, 64, 1), other)
    return jnp.where(side == half, own, other).astype(BF)


def stacked(block, heads):
    return jnp.concatenate([block[:, h * 128 : (h + 1) * 128] for h in range(heads)], axis=0)


def share_rows(place_ref, a_ref, b_ref, c_ref, d_ref, mine_ref, theirs_ref):
    half = place_ref[HALF]
    queries = queries_of((a_ref, b_ref, c_ref, d_ref), mine_ref.shape[1])
    top, bottom = queries[:GROUP], queries[GROUP:]
    mine_ref[...] = jnp.where(half == 0, top, bottom).astype(BF)
    theirs_ref[...] = jnp.where(half == 0, bottom, top).astype(BF)


def attend_pair(place_ref, lengths_ref, mine_ref, partner_ref, *refs):
    key_ref, value_ref, other_ref, own_ref, theirs_ref = refs
    half = place_ref[HALF]
    heads = mine_ref.shape[1] // 128
    blocks = [stacked(ref[...].astype(F32), heads) for ref in (mine_ref, partner_ref)]
    span = pl.ds(half * GROUP, GROUP)
    caches = (key_ref[span], other_ref[0], value_ref[span], other_ref[1])
    attended = group_attention(
        half, jnp.concatenate(blocks, axis=0), 2 * heads, lengths_ref, half * GROUP, caches
    )
    for index, out_ref in enumerate((own_ref, theirs_ref)):
        for h in range(heads):
            start = (index * heads + h) * GROUP
            out_ref[:, h * 128 : (h + 1) * 128] = attended[start : start + GROUP]


def rejoin(place_ref, own_ref, received_ref, out_ref):
    half = place_ref[HALF]
    top = jnp.where(half == 0, own_ref[...], received_ref[...])
    bottom = jnp.where(half == 0, received_ref[...], own_ref[...])
    for target in range(4):
        out_ref[target, :GROUP] = top
        out_ref[target, GROUP:] = bottom


def attend(place_ref, lengths_ref, a_ref, b_ref, c_ref, d_ref, *refs):
    key_ref, value_ref, near_ref, far_ref, out_ref = refs
    half = place_ref[HALF]
    heads = out_ref.shape[2] // 128
    queries = queries_of((a_ref, b_ref, c_ref, d_ref), out_ref.shape[2])

    @pl.loop(0, 2)
    def _(distance):
        index = half ^ distance
        start = pl.multiple_of(index * GROUP, GROUP)
        mine = jnp.where(index == 0, queries[:GROUP], queries[GROUP:])
        others = [jnp.where(distance == 0, near_ref[k], far_ref[k]) for k in range(2)]
        caches = (key_ref[pl.ds(start, GROUP)], others[0], value_ref[pl.ds(start, GROUP)], others[1])
        attended = group_attention(half, stacked(mine, heads), heads, lengths_ref, start, caches)
        for h in range(heads):
            tile = attended[h * GROUP : (h + 1) * GROUP]
            for target in range(4):
                out_ref[target, pl.ds(start, GROUP), h * 128 : (h + 1) * 128] = tile


def emit(mirrored, place_ref, near_ref, far_ref, weight_ref, *refs):
    out_refs, held = refs[:8], refs[8]
    y, z = place_ref[Y], place_ref[Z]
    rows = near_ref.shape[1]
    for side, ref in enumerate((near_ref, far_ref)):
        for step in range(4):
            start = (4 * side + step) * rows
            held[start : start + rows] = ref[place_ref[X] ^ step]
    for half, depths in enumerate(((1, 2), (3, 0))):
        for step in range(4):
            columns = []
            for depth in depths:
                column = z ^ depth ^ 3 if mirrored else z ^ depth
                start = pl.multiple_of(((y ^ step) * 4 + column) * 128, 128)
                columns.append(weight_ref[:, pl.ds(start, 128)])
            product = jnp.dot(
                held[...], jnp.concatenate(columns, axis=1), preferred_element_type=F32
            ).astype(BF)
            out_refs[4 * half + step][0] = product[:, :128]
            out_refs[4 * half + step][1] = product[:, 128:]


def merge(*refs):
    sources, targets = refs[:4], refs[4:]
    for index, target in enumerate(targets):
        total = sources[0][index].astype(F32)
        for source in sources[1:]:
            total += source[index].astype(F32)
        target[...] = total.astype(BF)


def updated(sources, state):
    total = sources[0][...].astype(F32)
    for source in sources[1:]:
        total += source[...].astype(F32)
    total = total.astype(BF).astype(F32)
    return (state.astype(F32) + total).astype(BF)


def merge_state(*refs):
    sources, state_ref, out_ref = refs[:4], refs[4], refs[5]
    out_ref[...] = updated(sources, state_ref[...])


def merge_last(place_ref, *refs):
    sources, state_ref, first_ref, out_ref = refs[:4], refs[4], refs[5], refs[6]
    result = updated(sources, state_ref[...]).astype(F32)
    result = jnp.where(place_ref[SECTION] == 0, first_ref[...].astype(F32), result).astype(BF)
    rows = out_ref.shape[1]
    for side in range(2):
        for step in range(4):
            owner = (place_ref[X] ^ step) * 2 + (place_ref[CORE] ^ side)
            start = (side * 4 + step) * rows
            out_ref[owner] = result[start : start + rows]


def lay_out(place_ref, *refs):
    y, z = place_ref[Y], place_ref[Z]
    out_ref = refs[-1]
    mirror = jnp.where(place_ref[SECTION] == 0, 0, 3)
    for step, ref in enumerate(refs[:-1]):
        for depth in range(4):
            index = (y ^ step) * 4 + (z ^ depth ^ mirror)
            for part in range(8):
                start = pl.multiple_of(index * 128 + part * 2048, 128)
                out_ref[:, pl.ds(start, 128)] = ref[depth, part]


def row_half(index, key, value):
    halves = [
        lax.dynamic_index_in_dim(c.reshape(2, GROUP, *c.shape[1:]), index, 0, keepdims=False)
        for c in (key, value)
    ]
    return jnp.stack(halves)


def spread(piece):
    return gathered(jnp.stack(gathered(piece, DEPTH)), "y")


def reduced(near, far):
    rows, wide = near.shape
    block = jax.ShapeDtypeStruct((rows // 4, wide), BF)
    sums = call(add_cores, [block] * 4, (near, moved(far, "c", 1)), name="add_cores")
    return [moved(s, "x", step) for step, s in enumerate(sums)]


def traded(blocks, axes):
    return lax.all_to_all(blocks, axes, split_axis=0, concat_axis=0, tiled=True)


def output(mirrored, attended, place, out_weight, awaited=None):
    near = traded(attended, "x")
    rows, wide = 8 * near.shape[1], near.shape[2]
    parts = call(
        functools.partial(emit, mirrored),
        [jax.ShapeDtypeStruct((2, rows, 128), BF)] * 8,
        (place, near, moved(near, "c", 1), out_weight),
        flops=2 * rows * wide * out_weight.shape[1],
        scratch=[pltpu.VMEM((rows, wide), BF)],
        name="emit",
    )
    parts = [moved(p, "y", step % 4) for step, p in enumerate(parts)]
    if awaited is not None:
        parts[4], awaited = lax.optimization_barrier((parts[4], awaited))
    share = jax.ShapeDtypeStruct((rows, 128), BF)
    one, two = call(merge, [share] * 2, parts[:4], name="merge")
    received = [moved(one, DEPTH, 1), moved(two, DEPTH, 2)]
    three, own = call(merge, [share] * 2, parts[4:], name="merge")
    return [own, *received, moved(three, DEPTH, 3)], awaited


def body(hidden, query_weight, out_weight, key_cache, value_cache, cache_lengths):
    place = jnp.stack([lax.axis_index(a) for a in ("y", DEPTH, "zl", "s", "x", "c")])
    place = place.astype(jnp.int32)
    rows, wide = hidden.shape
    part = wide // 8
    place = lax.optimization_barrier(place)
    query_weight, out_weight = query_weight[0], out_weight[0]
    key = jnp.swapaxes(key_cache[0], 1, 2)
    value = jnp.swapaxes(value_cache[0], 1, 2)
    half = lax.axis_index("zl").astype(jnp.int32)
    place, half = lax.optimization_barrier((place, half))
    near_half = moved(row_half(1 - half, key, value), "zl", 1)
    sent = call(
        arrange,
        [jax.ShapeDtypeStruct((2, rows, part), BF)] * 4,
        (place, hidden),
        name="arrange",
    )
    blocks = [moved(b, "x", step) for step, b in enumerate(sent)]
    other = call(pick, jax.ShapeDtypeStruct((4, rows, part), BF), blocks, name="pick")
    other = moved(other, "c", 1)
    partial = jax.ShapeDtypeStruct((4 * rows, query_weight.shape[1] + 128), BF)
    share = jax.ShapeDtypeStruct((8 * rows, 128), BF)
    held = pltpu.VMEM((8 * rows, part), BF)
    flops = 16 * rows * query_weight.shape[0] * query_weight.shape[1]
    near, far, state = call(
        project_rows,
        [partial, partial, share],
        (place, *blocks, other, query_weight),
        flops=flops,
        scratch=[held],
        name="project_rows",
    )
    far, near_half = lax.optimization_barrier((far, near_half))
    sums = reduced(near, far)
    query = jax.ShapeDtypeStruct((GROUP, query_weight.shape[1]), BF)
    mine, theirs = call(share_rows, [query, query], (place, *sums), name="share_rows")
    copies = jax.ShapeDtypeStruct((4, rows, query_weight.shape[1]), BF)
    own, sent = call(
        attend_pair,
        [query, query],
        (place, cache_lengths, mine, moved(theirs, "zl", 1), key, value, near_half),
        flops=8 * 8 * rows * 2048 * 256,
        name="attend_pair",
    )
    attended = call(
        rejoin,
        copies,
        (place, own, moved(sent, "zl", 1)),
        name="rejoin",
    )
    half, attended = lax.optimization_barrier((half, attended))
    far_half = moved(row_half(half, key, value), "zl", 1)
    parts, far_half = output(False, attended, place, out_weight, far_half)
    first = call(merge_state, share, (*parts, state), name="merge_state")

    arrived = moved(first, ("s", *DEPTH), 7)
    near, far = call(
        project_columns,
        [partial, partial],
        (place, *spread(arrived), query_weight),
        flops=flops,
        scratch=[held],
        name="project_columns",
    )
    attended = call(
        attend,
        copies,
        (
            place,
            cache_lengths,
            *reduced(near, far),
            *(key, value, near_half, far_half),
        ),
        flops=8 * 8 * rows * 2048 * 256,
        name="attend",
    )
    parts, _ = output(True, attended, place, out_weight)
    result = call(
        merge_last,
        jax.ShapeDtypeStruct((8, rows, 128), BF),
        (place, *parts, arrived, first),
        name="merge_last",
    )
    result = traded(result, DP)
    out = call(
        lay_out, jax.ShapeDtypeStruct((rows, wide), BF), (place, *spread(result)), name="lay_out"
    )
    return out[None]


def solution(mesh):
    fine = Mesh(mesh.devices.reshape(2, 4, 2, 4, 2, 2), ("s", "x", "c", "y", "zh", "zl"))
    in_specs = (
        P(DP, None),
        P("s", DP, TENSOR),
        P("s", TENSOR, DP),
        P("s", DP, None, TENSOR),
        P("s", DP, None, TENSOR),
        P(DP),
    )
    out_specs = P("s", DP, None)
    return jax.shard_map(body, mesh=fine, in_specs=in_specs, out_specs=out_specs, check_vma=False)
```

profile of v0, /device:TPU:1, one launch (start us, length us, event | category | flops | bytes accessed | tf_op | source)
XLA Modules:
  0.0 204.0 jit_solution(17486264102665796547)
XLA Ops:
  1.6 2.6 %collective-permute-start.4 = (bf16[2,16,64,256]{3,2,1,0:T(8,128)(2,1)S(1)}, bf16[2,16,64,256]{3,2,1,0:T(8,128)(2,1)S(1)}, u32[]{:S(2)}, u32[]{:S(2)}) collective-permute-start(bf16[2,16,64,256]{3,2,1,0:T(8,128)(2,1)S(1)} %pad_maximum_fusion), channel_id=1, source_target_pairs={{0,1},{1,0},{2,3},{3,2},{4,5},{5,4},{6,7},{7,6},{8,9},{9,8},{10,11... | collective-permute-start | bytes 3145736 | tf_op jit(solution)/shard_map/ppermute | solution.py:44
  6.1 2.5 %collective-permute-start.1 = (bf16[2,32,2048]{2,1,0:T(8,128)(2,1)S(1)}, bf16[2,32,2048]{2,1,0:T(8,128)(2,1)S(1)}, u32[]{:S(2)}, u32[]{:S(2)}) collective-permute-start(bf16[2,32,2048]{2,1,0:T(8,128)(2,1)S(1)} %get-tuple-element.62), channel_id=1, source_target_pairs={{0,64},{32,96},{64,0},{96,32},{1,65},{33,97},{65,1},{97,33},{2,66}... | collective-permute-start | bytes 786440 | tf_op jit(solution)/shard_map/ppermute | solution.py:44
  8.8 3.0 %collective-permute-done.refs_1_.b_ref = bf16[2,32,2048]{2,1,0:T(8,128)(2,1)S(1)} collective-permute-done((bf16[2,32,2048]{2,1,0:T(8,128)(2,1)S(1)}, bf16[2,32,2048]{2,1,0:T(8,128)(2,1)S(1)}, u32[]{:S(2)}, u32[]{:S(2)}) %collective-permute-start) | collective-permute-done | bytes 262176 | tf_op jit(solution)/shard_map/ppermute | solution.py:44
  11.8 7.9 %collective-permute-done.1.refs_2_.c_ref = bf16[2,32,2048]{2,1,0:T(8,128)(2,1)S(1)} collective-permute-done((bf16[2,32,2048]{2,1,0:T(8,128)(2,1)S(1)}, bf16[2,32,2048]{2,1,0:T(8,128)(2,1)S(1)}, u32[]{:S(2)}, u32[]{:S(2)}) %collective-permute-start.1) | collective-permute-done | bytes 262176 | tf_op jit(solution)/shard_map/ppermute | solution.py:44
  30.9 2.5 %collective-permute-start.7 = (bf16[32,1152]{1,0:T(8,128)(2,1)S(1)}, bf16[32,1152]{1,0:T(8,128)(2,1)S(1)}, u32[]{:S(2)}, u32[]{:S(2)}) collective-permute-start(bf16[32,1152]{1,0:T(8,128)(2,1)S(1)} %get-tuple-element.69), channel_id=1, source_target_pairs={{0,64},{32,96},{64,0},{96,32},{1,65},{33,97},{65,1},{97,33},{2,66}... | collective-permute-start | bytes 221192 | tf_op jit(solution)/shard_map/ppermute | solution.py:44
  33.8 2.8 %collective-permute-done.7.c_ref = bf16[32,1152]{1,0:T(8,128)(2,1)S(1)} collective-permute-done((bf16[32,1152]{1,0:T(8,128)(2,1)S(1)}, bf16[32,1152]{1,0:T(8,128)(2,1)S(1)}, u32[]{:S(2)}, u32[]{:S(2)}) %collective-permute-start.7) | collective-permute-done | bytes 73760 | tf_op jit(solution)/shard_map/ppermute | solution.py:44
  49.2 8.1 %all_to_all.15.near_ref = bf16[4,32,1024]{2,1,0:T(8,128)(2,1)S(1)} all-to-all(bf16[4,32,1024]{2,1,0:T(8,128)(2,1)S(1)} %rejoin.1), channel_id=1, replica_groups=mesh['s'=2,'x'=4,'c'=2,'y'=4,'zh'=2,'zl'=2] {'x'}, dimensions={0} | all-to-all | bytes 524288 | tf_op jit(solution)/shard_map/all_to_all | solution.py:322
  57.3 5.2 %collective-permute-start.11 = (bf16[4,32,1024]{2,1,0:T(8,128)(2,1)S(1)}, bf16[4,32,1024]{2,1,0:T(8,128)(2,1)S(1)}, u32[]{:S(2)}, u32[]{:S(2)}) collective-permute-start(bf16[4,32,1024]{2,1,0:T(8,128)(2,1)S(1)} %all_to_all.15.near_ref), channel_id=1, source_target_pairs={{0,16},{16,0},{1,17},{17,1},{2,18},{18,2},{3,19},{19,3},{4,20},{20... | collective-permute-start | bytes 786440 | tf_op jit(solution)/shard_map/ppermute | solution.py:44
  67.2 2.6 %collective-permute-start.17 = (bf16[2,256,128]{2,1,0:T(8,128)(2,1)S(1)}, bf16[2,256,128]{2,1,0:T(8,128)(2,1)S(1)}, u32[]{:S(2)}, u32[]{:S(2)}) collective-permute-start(bf16[2,256,128]{2,1,0:T(8,128)(2,1)S(1)} %get-tuple-element.86), channel_id=1, source_target_pairs={{0,8},{4,12},{8,0},{12,4},{1,9},{5,13},{9,1},{13,5},{2,10},{6,14},... | collective-permute-start | bytes 393224 | tf_op jit(solution)/shard_map/ppermute | solution.py:44
  70.6 3.1 %collective-permute-start.14 = (bf16[2,256,128]{2,1,0:T(8,128)(2,1)S(1)}, bf16[2,256,128]{2,1,0:T(8,128)(2,1)S(1)}, u32[]{:S(2)}, u32[]{:S(2)}) collective-permute-start(bf16[2,256,128]{2,1,0:T(8,128)(2,1)S(1)} %get-tuple-element.81), channel_id=1, source_target_pairs={{0,8},{4,12},{8,0},{12,4},{1,9},{5,13},{9,1},{13,5},{2,10},{6,14},... | collective-permute-start | bytes 393224 | tf_op jit(solution)/shard_map/ppermute | solution.py:44
  78.9 3.0 %collective-permute-start.20 = (bf16[256,128]{1,0:T(8,128)(2,1)S(1)}, bf16[256,128]{1,0:T(8,128)(2,1)S(1)}, u32[]{:S(2)}, u32[]{:S(2)}) collective-permute-start(bf16[256,128]{1,0:T(8,128)(2,1)S(1)} %get-tuple-element.89), channel_id=1, source_target_pairs={{0,2},{1,3},{2,0},{3,1},{4,6},{5,7},{6,4},{7,5},{8,10},{9,11},{10,... | collective-permute-start | bytes 196616 | tf_op jit(solution)/shard_map/ppermute | solution.py:44
  81.8 2.7 %collective-permute-done.15.refs_3_ = bf16[2,256,128]{2,1,0:T(8,128)(2,1)S(1)} collective-permute-done((bf16[2,256,128]{2,1,0:T(8,128)(2,1)S(1)}, bf16[2,256,128]{2,1,0:T(8,128)(2,1)S(1)}, u32[]{:S(2)}, u32[]{:S(2)}) %collective-permute-start.15) | collective-permute-done | bytes 131104 | tf_op jit(solution)/shard_map/ppermute | solution.py:44
  84.6 3.0 %collective-permute-start.21 = (bf16[256,128]{1,0:T(8,128)(2,1)S(1)}, bf16[256,128]{1,0:T(8,128)(2,1)S(1)}, u32[]{:S(2)}, u32[]{:S(2)}) collective-permute-start(bf16[256,128]{1,0:T(8,128)(2,1)S(1)} %get-tuple-element.90), channel_id=1, source_target_pairs={{0,3},{1,2},{2,1},{3,0},{4,7},{5,6},{6,5},{7,4},{8,11},{9,10},{10,... | collective-permute-start | bytes 196616 | tf_op jit(solution)/shard_map/ppermute | solution.py:44
  89.7 4.9 %collective-permute-start.22 = (bf16[256,128]{1,0:T(8,128)(2,1)S(1)}, bf16[256,128]{1,0:T(8,128)(2,1)S(1)}, u32[]{:S(2)}, u32[]{:S(2)}) collective-permute-start(bf16[256,128]{1,0:T(8,128)(2,1)S(1)} %merge_state.1.refs_5_), channel_id=1, source_target_pairs={{0,131},{1,130},{2,129},{3,128},{128,3},{129,2},{130,1},{131,0},{4... | collective-permute-start | bytes 196616 | tf_op jit(solution)/shard_map/ppermute | solution.py:44
  104.4 3.0 %collective-permute-start.26 = (bf16[4,256,128]{2,1,0:T(8,128)(2,1)S(1)}, bf16[4,256,128]{2,1,0:T(8,128)(2,1)S(1)}, u32[]{:S(2)}, u32[]{:S(2)}) collective-permute-start(bf16[4,256,128]{2,1,0:T(8,128)(2,1)S(1)} %pad_maximum_fusion.2.a_ref), channel_id=1, source_target_pairs={{0,4},{4,0},{8,12},{12,8},{1,5},{5,1},{9,13},{13,9},{2,6},{6,2},{1... | collective-permute-start | bytes 786440 | tf_op jit(solution)/shard_map/ppermute | solution.py:44
  107.4 10.8 %collective-permute-done.28.d_ref = bf16[4,256,128]{2,1,0:T(8,128)(2,1)S(1)} collective-permute-done((bf16[4,256,128]{2,1,0:T(8,128)(2,1)S(1)}, bf16[4,256,128]{2,1,0:T(8,128)(2,1)S(1)}, u32[]{:S(2)}, u32[]{:S(2)}) %collective-permute-start.28) | collective-permute-done | bytes 262176 | tf_op jit(solution)/shard_map/ppermute | solution.py:44
  118.2 2.6 %project_columns.1 = (bf16[128,1152]{1,0:T(8,128)(2,1)S(1)}, bf16[128,1152]{1,0:T(8,128)(2,1)S(1)}) custom-call(s32[6]{0:T(128)S(1)} %stack.67.place_ref, bf16[4,256,128]{2,1,0:T(8,128)(2,1)S(1)} %pad_maximum_fusion.2.a_ref, bf16[4,256,128]{2,1,0:T(8,128)(2,1)S(1)} %collective-permute-done.26.b_ref, bf16[4,256,128]{2,1,0:T(8,128)(2,1)S(1)} %collective-permute-done.27.c_ref, ...), custom_call_target="tpu_custom_call" | custom-call | flops 1073741824 | bytes 5832728 | tf_op jit(solution)/shard_map/project_columns/pallas_call | solution.py:26
  131.3 3.1 %attend.1 = bf16[4,32,1024]{2,1,0:T(8,128)(2,1)S(1)} custom-call(s32[6]{0:T(128)S(1)} %stack.67.place_ref, s32[32]{0:T(128)S(1)} %copy-done.6, bf16[32,1152]{1,0:T(8,128)(2,1)S(1)} %get-tuple-element.94.a_ref, bf16[32,1152]{1,0:T(8,128)(2,1)S(1)} %collective-permute-done.30.b_ref, bf16[32,1152]{1,0:T(8,128)(2,1)S(1)} %collective-permute-done.31.c_ref, ...), custom_call_target="tpu_custom_call" | custom-call | flops 1073741824 | bytes 4751512 | tf_op jit(solution)/shard_map/attend/pallas_call | solution.py:26
  134.5 8.6 %all_to_all.16.near_ref = bf16[4,32,1024]{2,1,0:T(8,128)(2,1)S(1)} all-to-all(bf16[4,32,1024]{2,1,0:T(8,128)(2,1)S(1)} %attend.1), channel_id=1, replica_groups=mesh['s'=2,'x'=4,'c'=2,'y'=4,'zh'=2,'zl'=2] {'x'}, dimensions={0} | all-to-all | bytes 524288 | tf_op jit(solution)/shard_map/all_to_all | solution.py:322
  143.1 3.0 %collective-permute-start.33 = (bf16[4,32,1024]{2,1,0:T(8,128)(2,1)S(1)}, bf16[4,32,1024]{2,1,0:T(8,128)(2,1)S(1)}, u32[]{:S(2)}, u32[]{:S(2)}) collective-permute-start(bf16[4,32,1024]{2,1,0:T(8,128)(2,1)S(1)} %all_to_all.16.near_ref), channel_id=1, source_target_pairs={{0,16},{16,0},{1,17},{17,1},{2,18},{18,2},{3,19},{19,3},{4,20},{20... | collective-permute-start | bytes 786440 | tf_op jit(solution)/shard_map/ppermute | solution.py:44
  170.4 9.6 %all_to_all.17 = bf16[8,32,128]{2,1,0:T(8,128)(2,1)S(1)} all-to-all(bf16[8,32,128]{2,1,0:T(8,128)(2,1)S(1)} %merge_last.1), channel_id=1, replica_groups=mesh['s'=2,'x'=4,'c'=2,'y'=4,'zh'=2,'zl'=2] {'x','c'}, dimensions={0} | all-to-all | bytes 131072 | tf_op jit(solution)/shard_map/all_to_all | solution.py:322
  185.0 3.4 %collective-permute-done.44 = bf16[8,32,128]{2,1,0:T(8,128)(2,1)S(1)} collective-permute-done((bf16[8,32,128]{2,1,0:T(8,128)(2,1)S(1)}, bf16[8,32,128]{2,1,0:T(8,128)(2,1)S(1)}, u32[]{:S(2)}, u32[]{:S(2)}) %collective-permute-start.44) | collective-permute-done | bytes 65568 | tf_op jit(solution)/shard_map/ppermute | solution.py:44
  188.5 2.5 %collective-permute-start.48 = (bf16[4,8,32,128]{3,2,1,0:T(8,128)(2,1)S(1)}, bf16[4,8,32,128]{3,2,1,0:T(8,128)(2,1)S(1)}, u32[]{:S(2)}, u32[]{:S(2)}) collective-permute-start(bf16[4,8,32,128]{3,2,1,0:T(8,128)(2,1)S(1)} %pad_maximum_fusion.3.refs_0_), channel_id=1, source_target_pairs={{0,12},{4,8},{8,4},{12,0},{1,13},{5,9},{9,5},{13,1},{2,14},{6,10},... | collective-permute-start | bytes 786440 | tf_op jit(solution)/shard_map/ppermute | solution.py:44
  191.8 10.2 %collective-permute-done.48.refs_3_ = bf16[4,8,32,128]{3,2,1,0:T(8,128)(2,1)S(1)} collective-permute-done((bf16[4,8,32,128]{3,2,1,0:T(8,128)(2,1)S(1)}, bf16[4,8,32,128]{3,2,1,0:T(8,128)(2,1)S(1)}, u32[]{:S(2)}, u32[]{:S(2)}) %collective-permute-start.48) | collective-permute-done | bytes 262176 | tf_op jit(solution)/shard_map/ppermute | solution.py:44
  (118 shorter events, 93.0 us)
Async XLA Ops:
  1.6 26.5 %collective-permute-start.4 = (bf16[2,16,64,256]{3,2,1,0:T(8,128)(2,1)S(1)}, bf16[2,16,64,256]{3,2,1,0:T(8,128)(2,1)S(1)}, u32[]{:S(2)}, u32[]{:S(2)}) collective-permute-start(bf16[2,16,64,256]{3,2,1,0:T(8,128)(2,1)S(1)} %pad_maximum_fusion), channel_id=1, source_target_pairs={{0,1},{1,0},{2,3},{3,2},{4,5},{5,4},{6,7},{7,6},{8,9},{9,8},{10,11... | collective-permute-start | bytes 3145736 | tf_op jit(solution)/shard_map/ppermute | solution.py:44
  6.1 13.5 %collective-permute-start.1 = (bf16[2,32,2048]{2,1,0:T(8,128)(2,1)S(1)}, bf16[2,32,2048]{2,1,0:T(8,128)(2,1)S(1)}, u32[]{:S(2)}, u32[]{:S(2)}) collective-permute-start(bf16[2,32,2048]{2,1,0:T(8,128)(2,1)S(1)} %get-tuple-element.62), channel_id=1, source_target_pairs={{0,64},{32,96},{64,0},{96,32},{1,65},{33,97},{65,1},{97,33},{2,66}... | collective-permute-start | bytes 786440 | tf_op jit(solution)/shard_map/ppermute | solution.py:44
  8.6 13.4 %collective-permute-start.2 = (bf16[2,32,2048]{2,1,0:T(8,128)(2,1)S(1)}, bf16[2,32,2048]{2,1,0:T(8,128)(2,1)S(1)}, u32[]{:S(2)}, u32[]{:S(2)}) collective-permute-start(bf16[2,32,2048]{2,1,0:T(8,128)(2,1)S(1)} %get-tuple-element.63), channel_id=1, source_target_pairs={{0,96},{32,64},{64,32},{96,0},{1,97},{33,65},{65,33},{97,1},{2,98}... | collective-permute-start | bytes 786440 | tf_op jit(solution)/shard_map/ppermute | solution.py:44
  47.6 31.3 %collective-permute-start.12 = (bf16[2,16,64,256]{3,2,1,0:T(8,128)(2,1)S(1)}, bf16[2,16,64,256]{3,2,1,0:T(8,128)(2,1)S(1)}, u32[]{:S(2)}, u32[]{:S(2)}) collective-permute-start(bf16[2,16,64,256]{3,2,1,0:T(8,128)(2,1)S(1)} %pad_maximum_fusion.1), channel_id=1, source_target_pairs={{0,1},{1,0},{2,3},{3,2},{4,5},{5,4},{6,7},{7,6},{8,9},{9,8},{10,11... | collective-permute-start | bytes 3145736 | tf_op jit(solution)/shard_map/ppermute | solution.py:44
  67.2 8.7 %collective-permute-start.17 = (bf16[2,256,128]{2,1,0:T(8,128)(2,1)S(1)}, bf16[2,256,128]{2,1,0:T(8,128)(2,1)S(1)}, u32[]{:S(2)}, u32[]{:S(2)}) collective-permute-start(bf16[2,256,128]{2,1,0:T(8,128)(2,1)S(1)} %get-tuple-element.86), channel_id=1, source_target_pairs={{0,8},{4,12},{8,0},{12,4},{1,9},{5,13},{9,1},{13,5},{2,10},{6,14},... | collective-permute-start | bytes 393224 | tf_op jit(solution)/shard_map/ppermute | solution.py:44
  69.8 8.6 %collective-permute-start.18 = (bf16[2,256,128]{2,1,0:T(8,128)(2,1)S(1)}, bf16[2,256,128]{2,1,0:T(8,128)(2,1)S(1)}, u32[]{:S(2)}, u32[]{:S(2)}) collective-permute-start(bf16[2,256,128]{2,1,0:T(8,128)(2,1)S(1)} %get-tuple-element.87), channel_id=1, source_target_pairs={{0,12},{4,8},{8,4},{12,0},{1,13},{5,9},{9,5},{13,1},{2,14},{6,10},... | collective-permute-start | bytes 393224 | tf_op jit(solution)/shard_map/ppermute | solution.py:44
  69.9 11.9 %collective-permute-start.13 = (bf16[2,256,128]{2,1,0:T(8,128)(2,1)S(1)}, bf16[2,256,128]{2,1,0:T(8,128)(2,1)S(1)}, u32[]{:S(2)}, u32[]{:S(2)}) collective-permute-start(bf16[2,256,128]{2,1,0:T(8,128)(2,1)S(1)} %get-tuple-element.80), channel_id=1, source_target_pairs={{0,4},{4,0},{8,12},{12,8},{1,5},{5,1},{9,13},{13,9},{2,6},{6,2},{1... | collective-permute-start | bytes 393224 | tf_op jit(solution)/shard_map/ppermute | solution.py:44
  70.6 11.2 %collective-permute-start.14 = (bf16[2,256,128]{2,1,0:T(8,128)(2,1)S(1)}, bf16[2,256,128]{2,1,0:T(8,128)(2,1)S(1)}, u32[]{:S(2)}, u32[]{:S(2)}) collective-permute-start(bf16[2,256,128]{2,1,0:T(8,128)(2,1)S(1)} %get-tuple-element.81), channel_id=1, source_target_pairs={{0,8},{4,12},{8,0},{12,4},{1,9},{5,13},{9,1},{13,5},{2,10},{6,14},... | collective-permute-start | bytes 393224 | tf_op jit(solution)/shard_map/ppermute | solution.py:44
  75.9 8.6 %collective-permute-start.15 = (bf16[2,256,128]{2,1,0:T(8,128)(2,1)S(1)}, bf16[2,256,128]{2,1,0:T(8,128)(2,1)S(1)}, u32[]{:S(2)}, u32[]{:S(2)}) collective-permute-start(bf16[2,256,128]{2,1,0:T(8,128)(2,1)S(1)} %get-tuple-element.82), channel_id=1, source_target_pairs={{0,12},{4,8},{8,4},{12,0},{1,13},{5,9},{9,5},{13,1},{2,14},{6,10},... | collective-permute-start | bytes 393224 | tf_op jit(solution)/shard_map/ppermute | solution.py:44
  78.5 9.1 %collective-permute-start.19 = (bf16[256,128]{1,0:T(8,128)(2,1)S(1)}, bf16[256,128]{1,0:T(8,128)(2,1)S(1)}, u32[]{:S(2)}, u32[]{:S(2)}) collective-permute-start(bf16[256,128]{1,0:T(8,128)(2,1)S(1)} %get-tuple-element.88), channel_id=1, source_target_pairs={{0,1},{1,0},{2,3},{3,2},{4,5},{5,4},{6,7},{7,6},{8,9},{9,8},{10,11... | collective-permute-start | bytes 196616 | tf_op jit(solution)/shard_map/ppermute | solution.py:44
  78.9 8.8 %collective-permute-start.20 = (bf16[256,128]{1,0:T(8,128)(2,1)S(1)}, bf16[256,128]{1,0:T(8,128)(2,1)S(1)}, u32[]{:S(2)}, u32[]{:S(2)}) collective-permute-start(bf16[256,128]{1,0:T(8,128)(2,1)S(1)} %get-tuple-element.89), channel_id=1, source_target_pairs={{0,2},{1,3},{2,0},{3,1},{4,6},{5,7},{6,4},{7,5},{8,10},{9,11},{10,... | collective-permute-start | bytes 196616 | tf_op jit(solution)/shard_map/ppermute | solution.py:44
  89.7 7.3 %collective-permute-start.22 = (bf16[256,128]{1,0:T(8,128)(2,1)S(1)}, bf16[256,128]{1,0:T(8,128)(2,1)S(1)}, u32[]{:S(2)}, u32[]{:S(2)}) collective-permute-start(bf16[256,128]{1,0:T(8,128)(2,1)S(1)} %merge_state.1.refs_5_), channel_id=1, source_target_pairs={{0,131},{1,130},{2,129},{3,128},{128,3},{129,2},{130,1},{131,0},{4... | collective-permute-start | bytes 196616 | tf_op jit(solution)/shard_map/ppermute | solution.py:44
  104.0 14.1 %collective-permute-start.28 = (bf16[4,256,128]{2,1,0:T(8,128)(2,1)S(1)}, bf16[4,256,128]{2,1,0:T(8,128)(2,1)S(1)}, u32[]{:S(2)}, u32[]{:S(2)}) collective-permute-start(bf16[4,256,128]{2,1,0:T(8,128)(2,1)S(1)} %pad_maximum_fusion.2.a_ref), channel_id=1, source_target_pairs={{0,12},{4,8},{8,4},{12,0},{1,13},{5,9},{9,5},{13,1},{2,14},{6,10},... | collective-permute-start | bytes 786440 | tf_op jit(solution)/shard_map/ppermute | solution.py:44
  104.4 13.8 %collective-permute-start.27 = (bf16[4,256,128]{2,1,0:T(8,128)(2,1)S(1)}, bf16[4,256,128]{2,1,0:T(8,128)(2,1)S(1)}, u32[]{:S(2)}, u32[]{:S(2)}) collective-permute-start(bf16[4,256,128]{2,1,0:T(8,128)(2,1)S(1)} %pad_maximum_fusion.2.a_ref), channel_id=1, source_target_pairs={{0,8},{4,12},{8,0},{12,4},{1,9},{5,13},{9,1},{13,5},{2,10},{6,14},... | collective-permute-start | bytes 786440 | tf_op jit(solution)/shard_map/ppermute | solution.py:44
  104.4 13.8 %collective-permute-start.26 = (bf16[4,256,128]{2,1,0:T(8,128)(2,1)S(1)}, bf16[4,256,128]{2,1,0:T(8,128)(2,1)S(1)}, u32[]{:S(2)}, u32[]{:S(2)}) collective-permute-start(bf16[4,256,128]{2,1,0:T(8,128)(2,1)S(1)} %pad_maximum_fusion.2.a_ref), channel_id=1, source_target_pairs={{0,4},{4,0},{8,12},{12,8},{1,5},{5,1},{9,13},{13,9},{2,6},{6,2},{1... | collective-permute-start | bytes 786440 | tf_op jit(solution)/shard_map/ppermute | solution.py:44
  149.5 7.7 %collective-permute-start.35 = (bf16[2,256,128]{2,1,0:T(8,128)(2,1)S(1)}, bf16[2,256,128]{2,1,0:T(8,128)(2,1)S(1)}, u32[]{:S(2)}, u32[]{:S(2)}) collective-permute-start(bf16[2,256,128]{2,1,0:T(8,128)(2,1)S(1)} %get-tuple-element.101), channel_id=1, source_target_pairs={{0,8},{4,12},{8,0},{12,4},{1,9},{5,13},{9,1},{13,5},{2,10},{6,14},... | collective-permute-start | bytes 393224 | tf_op jit(solution)/shard_map/ppermute | solution.py:44
  150.9 8.6 %collective-permute-start.36 = (bf16[2,256,128]{2,1,0:T(8,128)(2,1)S(1)}, bf16[2,256,128]{2,1,0:T(8,128)(2,1)S(1)}, u32[]{:S(2)}, u32[]{:S(2)}) collective-permute-start(bf16[2,256,128]{2,1,0:T(8,128)(2,1)S(1)} %get-tuple-element.102), channel_id=1, source_target_pairs={{0,12},{4,8},{8,4},{12,0},{1,13},{5,9},{9,5},{13,1},{2,14},{6,10},... | collective-permute-start | bytes 393224 | tf_op jit(solution)/shard_map/ppermute | solution.py:44
  153.3 7.3 %collective-permute-start.37 = (bf16[2,256,128]{2,1,0:T(8,128)(2,1)S(1)}, bf16[2,256,128]{2,1,0:T(8,128)(2,1)S(1)}, u32[]{:S(2)}, u32[]{:S(2)}) collective-permute-start(bf16[2,256,128]{2,1,0:T(8,128)(2,1)S(1)} %get-tuple-element.105), channel_id=1, source_target_pairs={{0,4},{4,0},{8,12},{12,8},{1,5},{5,1},{9,13},{13,9},{2,6},{6,2},{1... | collective-permute-start | bytes 393224 | tf_op jit(solution)/shard_map/ppermute | solution.py:44
  153.3 9.3 %collective-permute-start.38 = (bf16[2,256,128]{2,1,0:T(8,128)(2,1)S(1)}, bf16[2,256,128]{2,1,0:T(8,128)(2,1)S(1)}, u32[]{:S(2)}, u32[]{:S(2)}) collective-permute-start(bf16[2,256,128]{2,1,0:T(8,128)(2,1)S(1)} %get-tuple-element.106), channel_id=1, source_target_pairs={{0,8},{4,12},{8,0},{12,4},{1,9},{5,13},{9,1},{13,5},{2,10},{6,14},... | collective-permute-start | bytes 393224 | tf_op jit(solution)/shard_map/ppermute | solution.py:44
  154.8 10.3 %collective-permute-start.39 = (bf16[2,256,128]{2,1,0:T(8,128)(2,1)S(1)}, bf16[2,256,128]{2,1,0:T(8,128)(2,1)S(1)}, u32[]{:S(2)}, u32[]{:S(2)}) collective-permute-start(bf16[2,256,128]{2,1,0:T(8,128)(2,1)S(1)} %get-tuple-element.107), channel_id=1, source_target_pairs={{0,12},{4,8},{8,4},{12,0},{1,13},{5,9},{9,5},{13,1},{2,14},{6,10},... | collective-permute-start | bytes 393224 | tf_op jit(solution)/shard_map/ppermute | solution.py:44
  181.1 7.3 %collective-permute-start.44 = (bf16[8,32,128]{2,1,0:T(8,128)(2,1)S(1)}, bf16[8,32,128]{2,1,0:T(8,128)(2,1)S(1)}, u32[]{:S(2)}, u32[]{:S(2)}) collective-permute-start(bf16[8,32,128]{2,1,0:T(8,128)(2,1)S(1)} %all_to_all.17), channel_id=1, source_target_pairs={{0,2},{1,3},{2,0},{3,1},{4,6},{5,7},{6,4},{7,5},{8,10},{9,11},{10,... | collective-permute-start | bytes 196616 | tf_op jit(solution)/shard_map/ppermute | solution.py:44
  188.5 13.6 %collective-permute-start.48 = (bf16[4,8,32,128]{3,2,1,0:T(8,128)(2,1)S(1)}, bf16[4,8,32,128]{3,2,1,0:T(8,128)(2,1)S(1)}, u32[]{:S(2)}, u32[]{:S(2)}) collective-permute-start(bf16[4,8,32,128]{3,2,1,0:T(8,128)(2,1)S(1)} %pad_maximum_fusion.3.refs_0_), channel_id=1, source_target_pairs={{0,12},{4,8},{8,4},{12,0},{1,13},{5,9},{9,5},{13,1},{2,14},{6,10},... | collective-permute-start | bytes 786440 | tf_op jit(solution)/shard_map/ppermute | solution.py:44
  191.0 11.1 %collective-permute-start.47 = (bf16[4,8,32,128]{3,2,1,0:T(8,128)(2,1)S(1)}, bf16[4,8,32,128]{3,2,1,0:T(8,128)(2,1)S(1)}, u32[]{:S(2)}, u32[]{:S(2)}) collective-permute-start(bf16[4,8,32,128]{3,2,1,0:T(8,128)(2,1)S(1)} %pad_maximum_fusion.3.refs_0_), channel_id=1, source_target_pairs={{0,8},{4,12},{8,0},{12,4},{1,9},{5,13},{9,1},{13,5},{2,10},{6,14},... | collective-permute-start | bytes 786440 | tf_op jit(solution)/shard_map/ppermute | solution.py:44
  191.0 11.2 %collective-permute-start.46 = (bf16[4,8,32,128]{3,2,1,0:T(8,128)(2,1)S(1)}, bf16[4,8,32,128]{3,2,1,0:T(8,128)(2,1)S(1)}, u32[]{:S(2)}, u32[]{:S(2)}) collective-permute-start(bf16[4,8,32,128]{3,2,1,0:T(8,128)(2,1)S(1)} %pad_maximum_fusion.3.refs_0_), channel_id=1, source_target_pairs={{0,4},{4,0},{8,12},{12,8},{1,5},{5,1},{9,13},{13,9},{2,6},{6,2},{1... | collective-permute-start | bytes 786440 | tf_op jit(solution)/shard_map/ppermute | solution.py:44
  (32 other events, 345.5 us)
where the time goes:
time: 205 us; the launch traced here: 204 us
  waiting for transfers between devices  81.5 us (40%)
  starting transfers between devices  74.7 us (36%)
  blocking collectives  26.3 us (13%)
  Pallas kernels  19.3 us (9%)
    ppermute x49, waiting for transfers between devices, moved(): return lax.ppermute(block, axes, pairs)  81.5 us
    ppermute x49, starting transfers between devices, moved(): return lax.ppermute(block, axes, pairs)  74.7 us
    all_to_all x3, blocking collectives, traded(): return lax.all_to_all(blocks, axes, split_axis=0, concat_axis=0, tiled=True)  26.3 us
    pallas_call x19, Pallas kernels, call(): pl.pallas_call(kernel, out_shape=out_shapes, in_specs=[SMEM if a.ndim ==...  19.3 us
  transfers between devices with their start and end apart: 49, of which 32 were waited for; matrix products, arithmetic and copies ran while one was open for 0% of the time, Pallas kernels for 3%

commit v1 on v0

--- a/solution.py
+++ b/solution.py
@@ -76,9 +76,8 @@
         pieces = jnp.where(lane == 0, high, jnp.where(lane == 1, middle, low))
         out_ref[:, width:] = jnp.where(lane < 3, pieces, 0.0).astype(BF)
 
-    @pl.loop(0, width // 512)
-    def _(tile):
-        span = pl.ds(pl.multiple_of(tile * 512, 512), 512)
+    for tile in range(width // 256):
+        span = slice(tile * 256, (tile + 1) * 256)
         product = jnp.dot(held[...], weight_ref[:, span], preferred_element_type=F32).astype(BF)
         near_ref[:, span] = product[:rows]
         far_ref[:, span] = product[rows:]
@@ -111,10 +110,19 @@
         out_ref[...] = (near_ref[span].astype(F32) + far_ref[span].astype(F32)).astype(BF)
 
 
+def add_cores_pair(place_ref, near_ref, far_ref, out_ref):
+    for step in range(4):
+        for part in range(2):
+            start = (2 * step + part) * GROUP
+            span = slice(start, start + GROUP)
+            total = near_ref[span].astype(F32) + far_ref[span].astype(F32)
+            out_ref[(place_ref[X] ^ step) * 2 + part] = total.astype(BF)
+
+
 def queries_of(sums, width):
-    total = sums[0][...].astype(F32)
+    total = sums[0].astype(F32)
     for block in sums[1:]:
-        total += block[...].astype(F32)
+        total += block.astype(F32)
     squares = total[:, width : width + 1] + total[:, width + 1 : width + 2]
     squares = squares + total[:, width + 2 : width + 3]
     return total[:, :width] * lax.rsqrt(squares / 16384.0 + 1e-05)
@@ -178,52 +186,43 @@
     return jnp.concatenate([block[:, h * 128 : (h + 1) * 128] for h in range(heads)], axis=0)
 
 
-def share_rows(place_ref, a_ref, b_ref, c_ref, d_ref, mine_ref, theirs_ref):
+def attend_pair(place_ref, lengths_ref, sums_ref, key_ref, value_ref, other_ref, out_ref):
     half = place_ref[HALF]
-    queries = queries_of((a_ref, b_ref, c_ref, d_ref), mine_ref.shape[1])
-    top, bottom = queries[:GROUP], queries[GROUP:]
-    mine_ref[...] = jnp.where(half == 0, top, bottom).astype(BF)
-    theirs_ref[...] = jnp.where(half == 0, bottom, top).astype(BF)
-
-
-def attend_pair(place_ref, lengths_ref, mine_ref, partner_ref, *refs):
-    key_ref, value_ref, other_ref, own_ref, theirs_ref = refs
-    half = place_ref[HALF]
-    heads = mine_ref.shape[1] // 128
-    blocks = [stacked(ref[...].astype(F32), heads) for ref in (mine_ref, partner_ref)]
-    span = pl.ds(half * GROUP, GROUP)
-    caches = (key_ref[span], other_ref[0], value_ref[span], other_ref[1])
+    width = out_ref.shape[2]
+    heads = width // 128
+    parts = [
+        queries_of([sums_ref[2 * source + part] for source in range(4)], width) for part in range(2)
+    ]
+    blocks = [stacked(part, heads) for part in parts]
+    caches = (key_ref[...], other_ref[0], value_ref[...], other_ref[1])
     attended = group_attention(
         half, jnp.concatenate(blocks, axis=0), 2 * heads, lengths_ref, half * GROUP, caches
     )
-    for index, out_ref in enumerate((own_ref, theirs_ref)):
+    for part in range(2):
         for h in range(heads):
-            start = (index * heads + h) * GROUP
-            out_ref[:, h * 128 : (h + 1) * 128] = attended[start : start + GROUP]
-
-
-def rejoin(place_ref, own_ref, received_ref, out_ref):
-    half = place_ref[HALF]
-    top = jnp.where(half == 0, own_ref[...], received_ref[...])
-    bottom = jnp.where(half == 0, received_ref[...], own_ref[...])
-    for target in range(4):
-        out_ref[target, :GROUP] = top
-        out_ref[target, GROUP:] = bottom
+            start = (part * heads + h) * GROUP
+            for target in range(4):
+                out_ref[2 * target + part, :, h * 128 : (h + 1) * 128] = attended[
+                    start : start + GROUP
+                ]
 
 
 def attend(place_ref, lengths_ref, a_ref, b_ref, c_ref, d_ref, *refs):
-    key_ref, value_ref, near_ref, far_ref, out_ref = refs
+    key_ref, value_ref, near_ref, far_key_ref, far_value_ref, out_ref = refs
     half = place_ref[HALF]
     heads = out_ref.shape[2] // 128
-    queries = queries_of((a_ref, b_ref, c_ref, d_ref), out_ref.shape[2])
+    sums = [ref[...] for ref in (a_ref, b_ref, c_ref, d_ref)]
+    queries = queries_of(sums, out_ref.shape[2])
 
     @pl.loop(0, 2)
     def _(distance):
         index = half ^ distance
         start = pl.multiple_of(index * GROUP, GROUP)
         mine = jnp.where(index == 0, queries[:GROUP], queries[GROUP:])
-        others = [jnp.where(distance == 0, near_ref[k], far_ref[k]) for k in range(2)]
-        caches = (key_ref[pl.ds(start, GROUP)], others[0], value_ref[pl.ds(start, GROUP)], others[1])
+        other_key = jnp.where(distance == 0, near_ref[0], far_key_ref[...])
+        other_value = jnp.where(distance == 0, near_ref[1], far_value_ref[...])
+        span = pl.ds(start, GROUP)
+        caches = (key_ref[span], other_key, value_ref[span], other_value)
         attended = group_attention(half, stacked(mine, heads), heads, lengths_ref, start, caches)
         for h in range(heads):
             tile = attended[h * GROUP : (h + 1) * GROUP]
@@ -299,12 +298,9 @@
                 out_ref[:, pl.ds(start, 128)] = ref[depth, part]
 
 
-def row_half(index, key, value):
-    halves = [
-        lax.dynamic_index_in_dim(c.reshape(2, GROUP, *c.shape[1:]), index, 0, keepdims=False)
-        for c in (key, value)
-    ]
-    return jnp.stack(halves)
+def row_half(index, cache):
+    halves = cache.reshape(2, GROUP, *cache.shape[1:])
+    return lax.dynamic_index_in_dim(halves, index, 0, keepdims=False)
 
 
 def spread(piece):
@@ -322,8 +318,7 @@
     return lax.all_to_all(blocks, axes, split_axis=0, concat_axis=0, tiled=True)
 
 
-def output(mirrored, attended, place, out_weight, awaited=None):
-    near = traded(attended, "x")
+def output(mirrored, near, place, out_weight, awaited=None):
     rows, wide = 8 * near.shape[1], near.shape[2]
     parts = call(
         functools.partial(emit, mirrored),
@@ -335,7 +330,7 @@
     )
     parts = [moved(p, "y", step % 4) for step, p in enumerate(parts)]
     if awaited is not None:
-        parts[4], awaited = lax.optimization_barrier((parts[4], awaited))
+        parts[0], awaited = lax.optimization_barrier((parts[0], awaited))
     share = jax.ShapeDtypeStruct((rows, 128), BF)
     one, two = call(merge, [share] * 2, parts[:4], name="merge")
     received = [moved(one, DEPTH, 1), moved(two, DEPTH, 2)]
@@ -354,7 +349,8 @@
     value = jnp.swapaxes(value_cache[0], 1, 2)
     half = lax.axis_index("zl").astype(jnp.int32)
     place, half = lax.optimization_barrier((place, half))
-    near_half = moved(row_half(1 - half, key, value), "zl", 1)
+    near_half = jnp.stack([row_half(1 - half, key), row_half(1 - half, value)])
+    near_half = moved(near_half, "zl", 1)
     sent = call(
         arrange,
         [jax.ShapeDtypeStruct((2, rows, part), BF)] * 4,
@@ -362,6 +358,8 @@
         name="arrange",
     )
     blocks = [moved(b, "x", step) for step, b in enumerate(sent)]
+    mine_key, mine_value = row_half(half, key), row_half(half, value)
+    mine_key, mine_value, blocks[1] = lax.optimization_barrier((mine_key, mine_value, blocks[1]))
     other = call(pick, jax.ShapeDtypeStruct((4, rows, part), BF), blocks, name="pick")
     other = moved(other, "c", 1)
     partial = jax.ShapeDtypeStruct((4 * rows, query_weight.shape[1] + 128), BF)
@@ -377,50 +375,52 @@
         name="project_rows",
     )
     far, near_half = lax.optimization_barrier((far, near_half))
-    sums = reduced(near, far)
-    query = jax.ShapeDtypeStruct((GROUP, query_weight.shape[1]), BF)
-    mine, theirs = call(share_rows, [query, query], (place, *sums), name="share_rows")
-    copies = jax.ShapeDtypeStruct((4, rows, query_weight.shape[1]), BF)
-    own, sent = call(
+    width = query_weight.shape[1]
+    sums = call(
+        add_cores_pair,
+        jax.ShapeDtypeStruct((8, GROUP, width + 128), BF),
+        (place, near, moved(far, "c", 1)),
+        name="add_cores_pair",
+    )
+    attended = call(
         attend_pair,
-        [query, query],
-        (place, cache_lengths, mine, moved(theirs, "zl", 1), key, value, near_half),
+        jax.ShapeDtypeStruct((8, GROUP, width), BF),
+        (place, cache_lengths, traded(sums, ("x", "zl")), mine_key, mine_value, near_half),
         flops=8 * 8 * rows * 2048 * 256,
         name="attend_pair",
     )
-    attended = call(
-        rejoin,
-        copies,
-        (place, own, moved(sent, "zl", 1)),
-        name="rejoin",
-    )
-    half, attended = lax.optimization_barrier((half, attended))
-    far_half = moved(row_half(half, key, value), "zl", 1)
-    parts, far_half = output(False, attended, place, out_weight, far_half)
+    attended = traded(attended, ("x", "zl")).reshape(4, rows, width)
+    mine_key, attended = lax.optimization_barrier((mine_key, attended))
+    far_key = moved(mine_key, "zl", 1)
+    parts, far_key = output(False, attended, place, out_weight, far_key)
     first = call(merge_state, share, (*parts, state), name="merge_state")
 
     arrived = moved(first, ("s", *DEPTH), 7)
+    chunk = jnp.stack(gathered(arrived, DEPTH))
+    chunk, mine_value = lax.optimization_barrier((chunk, mine_value))
+    chunks = gathered(chunk, "y")
+    far_value = moved(mine_value, "zl", 1)
     near, far = call(
         project_columns,
         [partial, partial],
-        (place, *spread(arrived), query_weight),
+        (place, *chunks, query_weight),
         flops=flops,
         scratch=[held],
         name="project_columns",
     )
     attended = call(
         attend,
-        copies,
+        jax.ShapeDtypeStruct((4, rows, width), BF),
         (
             place,
             cache_lengths,
             *reduced(near, far),
-            *(key, value, near_half, far_half),
+            *(key, value, near_half, far_key, far_value),
         ),
         flops=8 * 8 * rows * 2048 * 256,
         name="attend",
     )
-    parts, _ = output(True, attended, place, out_weight)
+    parts, _ = output(True, traded(attended, "x"), place, out_weight)
     result = call(
         merge_last,
         jax.ShapeDtypeStruct((8, rows, 128), BF),

time: 205 us -> 199 us (0.971)
  blocking collectives: 26.3 us -> 39.7 us
  waiting for transfers between devices: 81.5 us -> 68.6 us
  starting transfers between devices: 74.7 us -> 69.7 us
    all_to_all x3 -> x4, blocking collectives: 26.3 us -> 39.7 us  [traded(): return lax.all_to_all(blocks, axes, split_axis=0, concat_axis=0, tiled=True)]
    ppermute x49 -> x45, waiting for transfers between devices: 81.5 us -> 68.6 us  [moved(): return lax.ppermute(block, axes, pairs)]
    ppermute x49 -> x45, starting transfers between devices: 74.7 us -> 69.7 us  [moved(): return lax.ppermute(block, axes, pairs)]
    pallas_call x19 -> x17, Pallas kernels: 19.3 us -> 18 us  [call(): pl.pallas_call(kernel, out_shape=out_shapes, in_specs=[SMEM if a.ndim ==...]
  transfers between devices with their start and end apart: 49 -> 45, of which waited for: 32 -> 29; matrix products, arithmetic and copies ran while one was open for 0% -> 0% of each run, Pallas kernels for 3% -> 4%
where the time goes in v1:
time: 199 us; the launch traced here: 198 us
  starting transfers between devices  69.7 us (35%)
  waiting for transfers between devices  68.6 us (34%)
  blocking collectives  39.7 us (20%)
  Pallas kernels  18 us (9%)
  local copies, waits for them, and re-layouts  1.99 us (1%)
    ppermute x45, starting transfers between devices, moved(): return lax.ppermute(block, axes, pairs)  69.7 us
    ppermute x45, waiting for transfers between devices, moved(): return lax.ppermute(block, axes, pairs)  68.6 us
    all_to_all x4, blocking collectives, traded(): return lax.all_to_all(blocks, axes, split_axis=0, concat_axis=0, tiled=True)  39.7 us
    pallas_call x17, Pallas kernels, call(): pl.pallas_call(kernel, out_shape=out_shapes, in_specs=[SMEM if a.ndim ==...  18 us
  transfers between devices with their start and end apart: 45, of which 29 were waited for; matrix products, arithmetic and copies ran while one was open for 0% of the time, Pallas kernels for 4%

profile of v1, /device:TPU:1, one launch (start us, length us, event | category | flops | bytes accessed | tf_op | source)
XLA Modules:
  0.0 198.3 jit_solution(15973719656328195987)
XLA Ops:
  2.1 2.6 %collective-permute-start.4 = (bf16[2,16,64,256]{3,2,1,0:T(8,128)(2,1)S(1)}, bf16[2,16,64,256]{3,2,1,0:T(8,128)(2,1)S(1)}, u32[]{:S(2)}, u32[]{:S(2)}) collective-permute-start(bf16[2,16,64,256]{3,2,1,0:T(8,128)(2,1)S(1)} %pad_maximum_fusion), channel_id=1, source_target_pairs={{0,1},{1,0},{2,3},{3,2},{4,5},{5,4},{6,7},{7,6},{8,9},{9,8},{10,11... | collective-permute-start | bytes 3145736 | tf_op jit(solution)/shard_map/ppermute | solution.py:44
  6.6 2.5 %collective-permute-start.1 = (bf16[2,32,2048]{2,1,0:T(8,128)(2,1)S(1)}, bf16[2,32,2048]{2,1,0:T(8,128)(2,1)S(1)}, u32[]{:S(2)}, u32[]{:S(2)}) collective-permute-start(bf16[2,32,2048]{2,1,0:T(8,128)(2,1)S(1)} %get-tuple-element.61), channel_id=1, source_target_pairs={{0,64},{32,96},{64,0},{96,32},{1,65},{33,97},{65,1},{97,33},{2,66}... | collective-permute-start | bytes 786440 | tf_op jit(solution)/shard_map/ppermute | solution.py:44
  9.2 3.0 %collective-permute-done.refs_1_.b_ref = bf16[2,32,2048]{2,1,0:T(8,128)(2,1)S(1)} collective-permute-done((bf16[2,32,2048]{2,1,0:T(8,128)(2,1)S(1)}, bf16[2,32,2048]{2,1,0:T(8,128)(2,1)S(1)}, u32[]{:S(2)}, u32[]{:S(2)}) %collective-permute-start) | collective-permute-done | bytes 262176 | tf_op jit(solution)/shard_map/ppermute | solution.py:44
  12.2 7.9 %collective-permute-done.1.refs_2_.c_ref = bf16[2,32,2048]{2,1,0:T(8,128)(2,1)S(1)} collective-permute-done((bf16[2,32,2048]{2,1,0:T(8,128)(2,1)S(1)}, bf16[2,32,2048]{2,1,0:T(8,128)(2,1)S(1)}, u32[]{:S(2)}, u32[]{:S(2)}) %collective-permute-start.1) | collective-permute-done | bytes 262176 | tf_op jit(solution)/shard_map/ppermute | solution.py:44
  30.6 12.2 %all_to_all.20.sums_ref = bf16[8,16,1152]{2,1,0:T(8,128)(2,1)S(1)} all-to-all(bf16[8,16,1152]{2,1,0:T(8,128)(2,1)S(1)} %add_cores_pair.1), channel_id=1, replica_groups=mesh['s'=2,'x'=4,'c'=2,'y'=4,'zh'=2,'zl'=2] {'x','zl'}, dimensions={0} | all-to-all | bytes 589824 | tf_op jit(solution)/shard_map/all_to_all | solution.py:318
  45.1 8.9 %all_to_all.21 = bf16[8,16,1024]{2,1,0:T(8,128)(2,1)S(1)} all-to-all(bf16[8,16,1024]{2,1,0:T(8,128)(2,1)S(1)} %attend_pair.1), channel_id=1, replica_groups=mesh['s'=2,'x'=4,'c'=2,'y'=4,'zh'=2,'zl'=2] {'x','zl'}, dimensions={0} | all-to-all | bytes 524288 | tf_op jit(solution)/shard_map/all_to_all | solution.py:318
  61.1 2.6 %collective-permute-start.8 = (bf16[2,256,128]{2,1,0:T(8,128)(2,1)S(1)}, bf16[2,256,128]{2,1,0:T(8,128)(2,1)S(1)}, u32[]{:S(2)}, u32[]{:S(2)}) collective-permute-start(bf16[2,256,128]{2,1,0:T(8,128)(2,1)S(1)} %get-tuple-element.71), channel_id=1, source_target_pairs={{0,8},{4,12},{8,0},{12,4},{1,9},{5,13},{9,1},{13,5},{2,10},{6,14},... | collective-permute-start | bytes 393224 | tf_op jit(solution)/shard_map/ppermute | solution.py:44
  64.5 3.1 %collective-permute-start.12 = (bf16[2,256,128]{2,1,0:T(8,128)(2,1)S(1)}, bf16[2,256,128]{2,1,0:T(8,128)(2,1)S(1)}, u32[]{:S(2)}, u32[]{:S(2)}) collective-permute-start(bf16[2,256,128]{2,1,0:T(8,128)(2,1)S(1)} %get-tuple-element.78), channel_id=1, source_target_pairs={{0,8},{4,12},{8,0},{12,4},{1,9},{5,13},{9,1},{13,5},{2,10},{6,14},... | collective-permute-start | bytes 393224 | tf_op jit(solution)/shard_map/ppermute | solution.py:44
  72.4 3.4 %collective-permute-start.16 = (bf16[256,128]{1,0:T(8,128)(2,1)S(1)}, bf16[256,128]{1,0:T(8,128)(2,1)S(1)}, u32[]{:S(2)}, u32[]{:S(2)}) collective-permute-start(bf16[256,128]{1,0:T(8,128)(2,1)S(1)} %get-tuple-element.82), channel_id=1, source_target_pairs={{0,3},{1,2},{2,1},{3,0},{4,7},{5,6},{6,5},{7,4},{8,11},{9,10},{10,... | collective-permute-start | bytes 196616 | tf_op jit(solution)/shard_map/ppermute | solution.py:44
  75.8 2.6 %collective-permute-done.13.refs_3_ = bf16[2,256,128]{2,1,0:T(8,128)(2,1)S(1)} collective-permute-done((bf16[2,256,128]{2,1,0:T(8,128)(2,1)S(1)}, bf16[2,256,128]{2,1,0:T(8,128)(2,1)S(1)}, u32[]{:S(2)}, u32[]{:S(2)}) %collective-permute-start.13) | collective-permute-done | bytes 131104 | tf_op jit(solution)/shard_map/ppermute | solution.py:44
  79.1 3.1 %collective-permute-start.15 = (bf16[256,128]{1,0:T(8,128)(2,1)S(1)}, bf16[256,128]{1,0:T(8,128)(2,1)S(1)}, u32[]{:S(2)}, u32[]{:S(2)}) collective-permute-start(bf16[256,128]{1,0:T(8,128)(2,1)S(1)} %get-tuple-element.81), channel_id=1, source_target_pairs={{0,2},{1,3},{2,0},{3,1},{4,6},{5,7},{6,4},{7,5},{8,10},{9,11},{10,... | collective-permute-start | bytes 196616 | tf_op jit(solution)/shard_map/ppermute | solution.py:44
  83.9 4.7 %collective-permute-start.17 = (bf16[256,128]{1,0:T(8,128)(2,1)S(1)}, bf16[256,128]{1,0:T(8,128)(2,1)S(1)}, u32[]{:S(2)}, u32[]{:S(2)}) collective-permute-start(bf16[256,128]{1,0:T(8,128)(2,1)S(1)} %merge_state.1.refs_5_), channel_id=1, source_target_pairs={{0,131},{1,130},{2,129},{3,128},{128,3},{129,2},{130,1},{131,0},{4... | collective-permute-start | bytes 196616 | tf_op jit(solution)/shard_map/ppermute | solution.py:44
  98.2 2.5 %collective-permute-start.21 = (bf16[4,256,128]{2,1,0:T(8,128)(2,1)S(1)}, bf16[4,256,128]{2,1,0:T(8,128)(2,1)S(1)}, u32[]{:S(2)}, u32[]{:S(2)}) collective-permute-start(bf16[4,256,128]{2,1,0:T(8,128)(2,1)S(1)} %pad_maximum_fusion.1.a_ref), channel_id=1, source_target_pairs={{0,4},{4,0},{8,12},{12,8},{1,5},{5,1},{9,13},{13,9},{2,6},{6,2},{1... | collective-permute-start | bytes 786440 | tf_op jit(solution)/shard_map/ppermute | solution.py:44
  101.0 6.4 %collective-permute-done.23.d_ref = bf16[4,256,128]{2,1,0:T(8,128)(2,1)S(1)} collective-permute-done((bf16[4,256,128]{2,1,0:T(8,128)(2,1)S(1)}, bf16[4,256,128]{2,1,0:T(8,128)(2,1)S(1)}, u32[]{:S(2)}, u32[]{:S(2)}) %collective-permute-start.23) | collective-permute-done | bytes 262176 | tf_op jit(solution)/shard_map/ppermute | solution.py:44
  110.0 6.0 %collective-permute-start.24 = (bf16[128,1152]{1,0:T(8,128)(2,1)S(1)}, bf16[128,1152]{1,0:T(8,128)(2,1)S(1)}, u32[]{:S(2)}, u32[]{:S(2)}) collective-permute-start(bf16[128,1152]{1,0:T(8,128)(2,1)S(1)} %get-tuple-element.86), channel_id=1, source_target_pairs={{0,16},{16,0},{1,17},{17,1},{2,18},{18,2},{3,19},{19,3},{4,20},{20... | collective-permute-start | bytes 884744 | tf_op jit(solution)/shard_map/ppermute | solution.py:44
  118.6 2.6 %collective-permute-start.27 = (bf16[32,1152]{1,0:T(8,128)(2,1)S(1)}, bf16[32,1152]{1,0:T(8,128)(2,1)S(1)}, u32[]{:S(2)}, u32[]{:S(2)}) collective-permute-start(bf16[32,1152]{1,0:T(8,128)(2,1)S(1)} %get-tuple-element.90), channel_id=1, source_target_pairs={{0,96},{32,64},{64,32},{96,0},{1,97},{33,65},{65,33},{97,1},{2,98}... | collective-permute-start | bytes 221192 | tf_op jit(solution)/shard_map/ppermute | solution.py:44
  124.2 3.2 %attend.1 = bf16[4,32,1024]{2,1,0:T(8,128)(2,1)S(1)} custom-call(s32[6]{0:T(128)S(1)} %stack.62.place_ref, s32[32]{0:T(128)S(1)} %copy-done.5, bf16[32,1152]{1,0:T(8,128)(2,1)S(1)} %get-tuple-element.87.a_ref, bf16[32,1152]{1,0:T(8,128)(2,1)S(1)} %collective-permute-done.25.b_ref, bf16[32,1152]{1,0:T(8,128)(2,1)S(1)} %collective-permute-done.26.c_ref, ...), custom_call_target="tpu_custom_call" | custom-call | flops 1073741824 | bytes 4751512 | tf_op jit(solution)/shard_map/attend/pallas_call | solution.py:26
  127.4 8.5 %all_to_all.22.near_ref = bf16[4,32,1024]{2,1,0:T(8,128)(2,1)S(1)} all-to-all(bf16[4,32,1024]{2,1,0:T(8,128)(2,1)S(1)} %attend.1), channel_id=1, replica_groups=mesh['s'=2,'x'=4,'c'=2,'y'=4,'zh'=2,'zl'=2] {'x'}, dimensions={0} | all-to-all | bytes 524288 | tf_op jit(solution)/shard_map/all_to_all | solution.py:318
  135.9 3.0 %collective-permute-start.29 = (bf16[4,32,1024]{2,1,0:T(8,128)(2,1)S(1)}, bf16[4,32,1024]{2,1,0:T(8,128)(2,1)S(1)}, u32[]{:S(2)}, u32[]{:S(2)}) collective-permute-start(bf16[4,32,1024]{2,1,0:T(8,128)(2,1)S(1)} %all_to_all.22.near_ref), channel_id=1, source_target_pairs={{0,16},{16,0},{1,17},{17,1},{2,18},{18,2},{3,19},{19,3},{4,20},{20... | collective-permute-start | bytes 786440 | tf_op jit(solution)/shard_map/ppermute | solution.py:44
  155.6 2.4 %collective-permute-done.35.refs_3_ = bf16[2,256,128]{2,1,0:T(8,128)(2,1)S(1)} collective-permute-done((bf16[2,256,128]{2,1,0:T(8,128)(2,1)S(1)}, bf16[2,256,128]{2,1,0:T(8,128)(2,1)S(1)}, u32[]{:S(2)}, u32[]{:S(2)}) %collective-permute-start.35) | collective-permute-done | bytes 131104 | tf_op jit(solution)/shard_map/ppermute | solution.py:44
  163.2 10.1 %all_to_all.23 = bf16[8,32,128]{2,1,0:T(8,128)(2,1)S(1)} all-to-all(bf16[8,32,128]{2,1,0:T(8,128)(2,1)S(1)} %merge_last.1), channel_id=1, replica_groups=mesh['s'=2,'x'=4,'c'=2,'y'=4,'zh'=2,'zl'=2] {'x','c'}, dimensions={0} | all-to-all | bytes 131072 | tf_op jit(solution)/shard_map/all_to_all | solution.py:318
  178.3 3.8 %collective-permute-done.40 = bf16[8,32,128]{2,1,0:T(8,128)(2,1)S(1)} collective-permute-done((bf16[8,32,128]{2,1,0:T(8,128)(2,1)S(1)}, bf16[8,32,128]{2,1,0:T(8,128)(2,1)S(1)}, u32[]{:S(2)}, u32[]{:S(2)}) %collective-permute-start.40) | collective-permute-done | bytes 65568 | tf_op jit(solution)/shard_map/ppermute | solution.py:44
  182.2 2.7 %collective-permute-start.44 = (bf16[4,8,32,128]{3,2,1,0:T(8,128)(2,1)S(1)}, bf16[4,8,32,128]{3,2,1,0:T(8,128)(2,1)S(1)}, u32[]{:S(2)}, u32[]{:S(2)}) collective-permute-start(bf16[4,8,32,128]{3,2,1,0:T(8,128)(2,1)S(1)} %pad_maximum_fusion.2.refs_0_), channel_id=1, source_target_pairs={{0,12},{4,8},{8,4},{12,0},{1,13},{5,9},{9,5},{13,1},{2,14},{6,10},... | collective-permute-start | bytes 786440 | tf_op jit(solution)/shard_map/ppermute | solution.py:44
  185.5 10.6 %collective-permute-done.44.refs_3_ = bf16[4,8,32,128]{3,2,1,0:T(8,128)(2,1)S(1)} collective-permute-done((bf16[4,8,32,128]{3,2,1,0:T(8,128)(2,1)S(1)}, bf16[4,8,32,128]{3,2,1,0:T(8,128)(2,1)S(1)}, u32[]{:S(2)}, u32[]{:S(2)}) %collective-permute-start.44) | collective-permute-done | bytes 262176 | tf_op jit(solution)/shard_map/ppermute | solution.py:44
  (104 shorter events, 79.9 us)
Async XLA Ops:
  2.1 26.1 %collective-permute-start.4 = (bf16[2,16,64,256]{3,2,1,0:T(8,128)(2,1)S(1)}, bf16[2,16,64,256]{3,2,1,0:T(8,128)(2,1)S(1)}, u32[]{:S(2)}, u32[]{:S(2)}) collective-permute-start(bf16[2,16,64,256]{3,2,1,0:T(8,128)(2,1)S(1)} %pad_maximum_fusion), channel_id=1, source_target_pairs={{0,1},{1,0},{2,3},{3,2},{4,5},{5,4},{6,7},{7,6},{8,9},{9,8},{10,11... | collective-permute-start | bytes 3145736 | tf_op jit(solution)/shard_map/ppermute | solution.py:44
  6.6 13.5 %collective-permute-start.1 = (bf16[2,32,2048]{2,1,0:T(8,128)(2,1)S(1)}, bf16[2,32,2048]{2,1,0:T(8,128)(2,1)S(1)}, u32[]{:S(2)}, u32[]{:S(2)}) collective-permute-start(bf16[2,32,2048]{2,1,0:T(8,128)(2,1)S(1)} %get-tuple-element.61), channel_id=1, source_target_pairs={{0,64},{32,96},{64,0},{96,32},{1,65},{33,97},{65,1},{97,33},{2,66}... | collective-permute-start | bytes 786440 | tf_op jit(solution)/shard_map/ppermute | solution.py:44
  9.0 13.4 %collective-permute-start.2 = (bf16[2,32,2048]{2,1,0:T(8,128)(2,1)S(1)}, bf16[2,32,2048]{2,1,0:T(8,128)(2,1)S(1)}, u32[]{:S(2)}, u32[]{:S(2)}) collective-permute-start(bf16[2,32,2048]{2,1,0:T(8,128)(2,1)S(1)} %get-tuple-element.62), channel_id=1, source_target_pairs={{0,96},{32,64},{64,32},{96,0},{1,97},{33,65},{65,33},{97,1},{2,98}... | collective-permute-start | bytes 786440 | tf_op jit(solution)/shard_map/ppermute | solution.py:44
  56.4 19.4 %collective-permute-start.10 = (bf16[16,64,256]{2,1,0:T(8,128)(2,1)S(1)}, bf16[16,64,256]{2,1,0:T(8,128)(2,1)S(1)}, u32[]{:S(2)}, u32[]{:S(2)}) collective-permute-start(bf16[16,64,256]{2,1,0:T(8,128)(2,1)S(1)} %get-tuple-element.75.key_ref), channel_id=1, source_target_pairs={{0,1},{1,0},{2,3},{3,2},{4,5},{5,4},{6,7},{7,6},{8,9},{9,8},{10,11... | collective-permute-start | bytes 1572872 | tf_op jit(solution)/shard_map/ppermute | solution.py:44
  61.1 8.7 %collective-permute-start.8 = (bf16[2,256,128]{2,1,0:T(8,128)(2,1)S(1)}, bf16[2,256,128]{2,1,0:T(8,128)(2,1)S(1)}, u32[]{:S(2)}, u32[]{:S(2)}) collective-permute-start(bf16[2,256,128]{2,1,0:T(8,128)(2,1)S(1)} %get-tuple-element.71), channel_id=1, source_target_pairs={{0,8},{4,12},{8,0},{12,4},{1,9},{5,13},{9,1},{13,5},{2,10},{6,14},... | collective-permute-start | bytes 393224 | tf_op jit(solution)/shard_map/ppermute | solution.py:44
  63.7 8.6 %collective-permute-start.9 = (bf16[2,256,128]{2,1,0:T(8,128)(2,1)S(1)}, bf16[2,256,128]{2,1,0:T(8,128)(2,1)S(1)}, u32[]{:S(2)}, u32[]{:S(2)}) collective-permute-start(bf16[2,256,128]{2,1,0:T(8,128)(2,1)S(1)} %get-tuple-element.72), channel_id=1, source_target_pairs={{0,12},{4,8},{8,4},{12,0},{1,13},{5,9},{9,5},{13,1},{2,14},{6,10},... | collective-permute-start | bytes 393224 | tf_op jit(solution)/shard_map/ppermute | solution.py:44
  63.7 12.0 %collective-permute-start.11 = (bf16[2,256,128]{2,1,0:T(8,128)(2,1)S(1)}, bf16[2,256,128]{2,1,0:T(8,128)(2,1)S(1)}, u32[]{:S(2)}, u32[]{:S(2)}) collective-permute-start(bf16[2,256,128]{2,1,0:T(8,128)(2,1)S(1)} %get-tuple-element.77), channel_id=1, source_target_pairs={{0,4},{4,0},{8,12},{12,8},{1,5},{5,1},{9,13},{13,9},{2,6},{6,2},{1... | collective-permute-start | bytes 393224 | tf_op jit(solution)/shard_map/ppermute | solution.py:44
  64.5 11.2 %collective-permute-start.12 = (bf16[2,256,128]{2,1,0:T(8,128)(2,1)S(1)}, bf16[2,256,128]{2,1,0:T(8,128)(2,1)S(1)}, u32[]{:S(2)}, u32[]{:S(2)}) collective-permute-start(bf16[2,256,128]{2,1,0:T(8,128)(2,1)S(1)} %get-tuple-element.78), channel_id=1, source_target_pairs={{0,8},{4,12},{8,0},{12,4},{1,9},{5,13},{9,1},{13,5},{2,10},{6,14},... | collective-permute-start | bytes 393224 | tf_op jit(solution)/shard_map/ppermute | solution.py:44
  69.8 8.6 %collective-permute-start.13 = (bf16[2,256,128]{2,1,0:T(8,128)(2,1)S(1)}, bf16[2,256,128]{2,1,0:T(8,128)(2,1)S(1)}, u32[]{:S(2)}, u32[]{:S(2)}) collective-permute-start(bf16[2,256,128]{2,1,0:T(8,128)(2,1)S(1)} %get-tuple-element.79), channel_id=1, source_target_pairs={{0,12},{4,8},{8,4},{12,0},{1,13},{5,9},{9,5},{13,1},{2,14},{6,10},... | collective-permute-start | bytes 393224 | tf_op jit(solution)/shard_map/ppermute | solution.py:44
  72.4 9.8 %collective-permute-start.16 = (bf16[256,128]{1,0:T(8,128)(2,1)S(1)}, bf16[256,128]{1,0:T(8,128)(2,1)S(1)}, u32[]{:S(2)}, u32[]{:S(2)}) collective-permute-start(bf16[256,128]{1,0:T(8,128)(2,1)S(1)} %get-tuple-element.82), channel_id=1, source_target_pairs={{0,3},{1,2},{2,1},{3,0},{4,7},{5,6},{6,5},{7,4},{8,11},{9,10},{10,... | collective-permute-start | bytes 196616 | tf_op jit(solution)/shard_map/ppermute | solution.py:44
  97.4 10.0 %collective-permute-start.23 = (bf16[4,256,128]{2,1,0:T(8,128)(2,1)S(1)}, bf16[4,256,128]{2,1,0:T(8,128)(2,1)S(1)}, u32[]{:S(2)}, u32[]{:S(2)}) collective-permute-start(bf16[4,256,128]{2,1,0:T(8,128)(2,1)S(1)} %pad_maximum_fusion.1.a_ref), channel_id=1, source_target_pairs={{0,12},{4,8},{8,4},{12,0},{1,13},{5,9},{9,5},{13,1},{2,14},{6,10},... | collective-permute-start | bytes 786440 | tf_op jit(solution)/shard_map/ppermute | solution.py:44
  97.8 9.6 %collective-permute-start.22 = (bf16[4,256,128]{2,1,0:T(8,128)(2,1)S(1)}, bf16[4,256,128]{2,1,0:T(8,128)(2,1)S(1)}, u32[]{:S(2)}, u32[]{:S(2)}) collective-permute-start(bf16[4,256,128]{2,1,0:T(8,128)(2,1)S(1)} %pad_maximum_fusion.1.a_ref), channel_id=1, source_target_pairs={{0,8},{4,12},{8,0},{12,4},{1,9},{5,13},{9,1},{13,5},{2,10},{6,14},... | collective-permute-start | bytes 786440 | tf_op jit(solution)/shard_map/ppermute | solution.py:44
  98.2 9.6 %collective-permute-start.21 = (bf16[4,256,128]{2,1,0:T(8,128)(2,1)S(1)}, bf16[4,256,128]{2,1,0:T(8,128)(2,1)S(1)}, u32[]{:S(2)}, u32[]{:S(2)}) collective-permute-start(bf16[4,256,128]{2,1,0:T(8,128)(2,1)S(1)} %pad_maximum_fusion.1.a_ref), channel_id=1, source_target_pairs={{0,4},{4,0},{8,12},{12,8},{1,5},{5,1},{9,13},{13,9},{2,6},{6,2},{1... | collective-permute-start | bytes 786440 | tf_op jit(solution)/shard_map/ppermute | solution.py:44
  100.8 20.5 %collective-permute-start.28 = (bf16[16,64,256]{2,1,0:T(8,128)(2,1)S(1)}, bf16[16,64,256]{2,1,0:T(8,128)(2,1)S(1)}, u32[]{:S(2)}, u32[]{:S(2)}) collective-permute-start(bf16[16,64,256]{2,1,0:T(8,128)(2,1)S(1)} %get-tuple-element.92.value_ref), channel_id=1, source_target_pairs={{0,1},{1,0},{2,3},{3,2},{4,5},{5,4},{6,7},{7,6},{8,9},{9,8},{10,11... | collective-permute-start | bytes 1572872 | tf_op jit(solution)/shard_map/ppermute | solution.py:44
  110.0 7.2 %collective-permute-start.24 = (bf16[128,1152]{1,0:T(8,128)(2,1)S(1)}, bf16[128,1152]{1,0:T(8,128)(2,1)S(1)}, u32[]{:S(2)}, u32[]{:S(2)}) collective-permute-start(bf16[128,1152]{1,0:T(8,128)(2,1)S(1)} %get-tuple-element.86), channel_id=1, source_target_pairs={{0,16},{16,0},{1,17},{17,1},{2,18},{18,2},{3,19},{19,3},{4,20},{20... | collective-permute-start | bytes 884744 | tf_op jit(solution)/shard_map/ppermute | solution.py:44
  142.3 7.7 %collective-permute-start.31 = (bf16[2,256,128]{2,1,0:T(8,128)(2,1)S(1)}, bf16[2,256,128]{2,1,0:T(8,128)(2,1)S(1)}, u32[]{:S(2)}, u32[]{:S(2)}) collective-permute-start(bf16[2,256,128]{2,1,0:T(8,128)(2,1)S(1)} %get-tuple-element.95), channel_id=1, source_target_pairs={{0,8},{4,12},{8,0},{12,4},{1,9},{5,13},{9,1},{13,5},{2,10},{6,14},... | collective-permute-start | bytes 393224 | tf_op jit(solution)/shard_map/ppermute | solution.py:44
  143.8 8.6 %collective-permute-start.32 = (bf16[2,256,128]{2,1,0:T(8,128)(2,1)S(1)}, bf16[2,256,128]{2,1,0:T(8,128)(2,1)S(1)}, u32[]{:S(2)}, u32[]{:S(2)}) collective-permute-start(bf16[2,256,128]{2,1,0:T(8,128)(2,1)S(1)} %get-tuple-element.96), channel_id=1, source_target_pairs={{0,12},{4,8},{8,4},{12,0},{1,13},{5,9},{9,5},{13,1},{2,14},{6,10},... | collective-permute-start | bytes 393224 | tf_op jit(solution)/shard_map/ppermute | solution.py:44
  146.2 7.9 %collective-permute-start.33 = (bf16[2,256,128]{2,1,0:T(8,128)(2,1)S(1)}, bf16[2,256,128]{2,1,0:T(8,128)(2,1)S(1)}, u32[]{:S(2)}, u32[]{:S(2)}) collective-permute-start(bf16[2,256,128]{2,1,0:T(8,128)(2,1)S(1)} %get-tuple-element.99), channel_id=1, source_target_pairs={{0,4},{4,0},{8,12},{12,8},{1,5},{5,1},{9,13},{13,9},{2,6},{6,2},{1... | collective-permute-start | bytes 393224 | tf_op jit(solution)/shard_map/ppermute | solution.py:44
  146.2 9.4 %collective-permute-start.34 = (bf16[2,256,128]{2,1,0:T(8,128)(2,1)S(1)}, bf16[2,256,128]{2,1,0:T(8,128)(2,1)S(1)}, u32[]{:S(2)}, u32[]{:S(2)}) collective-permute-start(bf16[2,256,128]{2,1,0:T(8,128)(2,1)S(1)} %get-tuple-element.100), channel_id=1, source_target_pairs={{0,8},{4,12},{8,0},{12,4},{1,9},{5,13},{9,1},{13,5},{2,10},{6,14},... | collective-permute-start | bytes 393224 | tf_op jit(solution)/shard_map/ppermute | solution.py:44
  147.7 10.3 %collective-permute-start.35 = (bf16[2,256,128]{2,1,0:T(8,128)(2,1)S(1)}, bf16[2,256,128]{2,1,0:T(8,128)(2,1)S(1)}, u32[]{:S(2)}, u32[]{:S(2)}) collective-permute-start(bf16[2,256,128]{2,1,0:T(8,128)(2,1)S(1)} %get-tuple-element.101), channel_id=1, source_target_pairs={{0,12},{4,8},{8,4},{12,0},{1,13},{5,9},{9,5},{13,1},{2,14},{6,10},... | collective-permute-start | bytes 393224 | tf_op jit(solution)/shard_map/ppermute | solution.py:44
  152.5 7.5 %collective-permute-start.38 = (bf16[256,128]{1,0:T(8,128)(2,1)S(1)}, bf16[256,128]{1,0:T(8,128)(2,1)S(1)}, u32[]{:S(2)}, u32[]{:S(2)}) collective-permute-start(bf16[256,128]{1,0:T(8,128)(2,1)S(1)} %get-tuple-element.104), channel_id=1, source_target_pairs={{0,3},{1,2},{2,1},{3,0},{4,7},{5,6},{6,5},{7,4},{8,11},{9,10},{10,... | collective-permute-start | bytes 196616 | tf_op jit(solution)/shard_map/ppermute | solution.py:44
  182.2 14.0 %collective-permute-start.44 = (bf16[4,8,32,128]{3,2,1,0:T(8,128)(2,1)S(1)}, bf16[4,8,32,128]{3,2,1,0:T(8,128)(2,1)S(1)}, u32[]{:S(2)}, u32[]{:S(2)}) collective-permute-start(bf16[4,8,32,128]{3,2,1,0:T(8,128)(2,1)S(1)} %pad_maximum_fusion.2.refs_0_), channel_id=1, source_target_pairs={{0,12},{4,8},{8,4},{12,0},{1,13},{5,9},{9,5},{13,1},{2,14},{6,10},... | collective-permute-start | bytes 786440 | tf_op jit(solution)/shard_map/ppermute | solution.py:44
  184.8 11.3 %collective-permute-start.43 = (bf16[4,8,32,128]{3,2,1,0:T(8,128)(2,1)S(1)}, bf16[4,8,32,128]{3,2,1,0:T(8,128)(2,1)S(1)}, u32[]{:S(2)}, u32[]{:S(2)}) collective-permute-start(bf16[4,8,32,128]{3,2,1,0:T(8,128)(2,1)S(1)} %pad_maximum_fusion.2.refs_0_), channel_id=1, source_target_pairs={{0,8},{4,12},{8,0},{12,4},{1,9},{5,13},{9,1},{13,5},{2,10},{6,14},... | collective-permute-start | bytes 786440 | tf_op jit(solution)/shard_map/ppermute | solution.py:44
  184.8 11.6 %collective-permute-start.42 = (bf16[4,8,32,128]{3,2,1,0:T(8,128)(2,1)S(1)}, bf16[4,8,32,128]{3,2,1,0:T(8,128)(2,1)S(1)}, u32[]{:S(2)}, u32[]{:S(2)}) collective-permute-start(bf16[4,8,32,128]{3,2,1,0:T(8,128)(2,1)S(1)} %pad_maximum_fusion.2.refs_0_), channel_id=1, source_target_pairs={{0,4},{4,0},{8,12},{12,8},{1,5},{5,1},{9,13},{13,9},{2,6},{6,2},{1... | collective-permute-start | bytes 786440 | tf_op jit(solution)/shard_map/ppermute | solution.py:44
  (27 other events, 309.2 us)

commit v2 on v1

--- a/solution.py
+++ b/solution.py
@@ -63,7 +63,7 @@
         out_ref[step] = ref[1] if len(ref.shape) == 3 else ref[...]
 
 
-def project(held, weight_ref, near_ref, far_ref):
+def project(held, weight_ref, near_ref, far_ref, unrolled):
     rows = near_ref.shape[0]
     width = weight_ref.shape[1]
     for start, out_ref in ((rows, far_ref), (0, near_ref)):
@@ -76,11 +76,19 @@
         pieces = jnp.where(lane == 0, high, jnp.where(lane == 1, middle, low))
         out_ref[:, width:] = jnp.where(lane < 3, pieces, 0.0).astype(BF)
 
-    for tile in range(width // 256):
-        span = slice(tile * 256, (tile + 1) * 256)
+    def multiply(span):
         product = jnp.dot(held[...], weight_ref[:, span], preferred_element_type=F32).astype(BF)
         near_ref[:, span] = product[:rows]
         far_ref[:, span] = product[rows:]
+
+    if unrolled:
+        for start in range(0, width, 256):
+            multiply(slice(start, start + 256))
+        return
+
+    @pl.loop(0, width // 512)
+    def _(tile):
+        multiply(pl.ds(pl.multiple_of(tile * 512, 512), 512))
 
 
 def project_rows(place_ref, a_ref, b_ref, c_ref, d_ref, other_ref, weight_ref, *refs):
@@ -91,7 +99,7 @@
         held[(step + 4) * rows : (step + 5) * rows] = other_ref[step]
     start = (place_ref[Y] * 4 + place_ref[Z]) * 128
     state_ref[...] = held[:, pl.ds(pl.multiple_of(start, 128), 128)]
-    project(held, weight_ref, near_ref, far_ref)
+    project(held, weight_ref, near_ref, far_ref, False)
 
 
 def project_columns(place_ref, a_ref, b_ref, c_ref, d_ref, weight_ref, near_ref, far_ref, held):
@@ -100,7 +108,7 @@
         for depth in range(4):
             index = (y ^ step) * 4 + (z ^ depth ^ 3)
             held[:, pl.ds(pl.multiple_of(index * 128, 128), 128)] = ref[depth]
-    project(held, weight_ref, near_ref, far_ref)
+    project(held, weight_ref, near_ref, far_ref, True)
 
 
 def add_cores(near_ref, far_ref, *out_refs):
@@ -210,9 +218,9 @@
 def attend(place_ref, lengths_ref, a_ref, b_ref, c_ref, d_ref, *refs):
     key_ref, value_ref, near_ref, far_key_ref, far_value_ref, out_ref = refs
     half = place_ref[HALF]
-    heads = out_ref.shape[2] // 128
+    heads = out_ref.shape[1] // 128
     sums = [ref[...] for ref in (a_ref, b_ref, c_ref, d_ref)]
-    queries = queries_of(sums, out_ref.shape[2])
+    queries = queries_of(sums, out_ref.shape[1])
 
     @pl.loop(0, 2)
     def _(distance):
@@ -226,8 +234,7 @@
         attended = group_attention(half, stacked(mine, heads), heads, lengths_ref, start, caches)
         for h in range(heads):
             tile = attended[h * GROUP : (h + 1) * GROUP]
-            for target in range(4):
-                out_ref[target, pl.ds(start, GROUP), h * 128 : (h + 1) * 128] = tile
+            out_ref[pl.ds(start, GROUP), h * 128 : (h + 1) * 128] = tile
 
 
 def emit(mirrored, place_ref, near_ref, far_ref, weight_ref, *refs):
@@ -237,7 +244,7 @@
     for side, ref in enumerate((near_ref, far_ref)):
         for step in range(4):
             start = (4 * side + step) * rows
-            held[start : start + rows] = ref[place_ref[X] ^ step]
+            held[start : start + rows] = ref[step if mirrored else place_ref[X] ^ step]
     for half, depths in enumerate(((1, 2), (3, 0))):
         for step in range(4):
             columns = []
@@ -410,7 +417,7 @@
     )
     attended = call(
         attend,
-        jax.ShapeDtypeStruct((4, rows, width), BF),
+        jax.ShapeDtypeStruct((rows, width), BF),
         (
             place,
             cache_lengths,
@@ -420,7 +427,8 @@
         flops=8 * 8 * rows * 2048 * 256,
         name="attend",
     )
-    parts, _ = output(True, traded(attended, "x"), place, out_weight)
+    near = call(pick, jax.ShapeDtypeStruct((4, rows, width), BF), gathered(attended, "x"), name="pick")
+    parts, _ = output(True, near, place, out_weight)
     result = call(
         merge_last,
         jax.ShapeDtypeStruct((8, rows, 128), BF),

time: 199 us -> 198 us (level)
  blocking collectives: 39.7 us -> 31.1 us
  waiting for transfers between devices: 68.6 us -> 72.6 us
  starting transfers between devices: 69.7 us -> 73.5 us
    all_to_all x4 -> x3, blocking collectives: 39.7 us -> 31.1 us  [traded(): return lax.all_to_all(blocks, axes, split_axis=0, concat_axis=0, tiled=True)]
    ppermute x45 -> x48, waiting for transfers between devices: 68.6 us -> 72.6 us  [moved(): return lax.ppermute(block, axes, pairs)]
    ppermute x45 -> x48, starting transfers between devices: 69.7 us -> 73.5 us  [moved(): return lax.ppermute(block, axes, pairs)]
    pallas_call x17 -> x18, Pallas kernels: 18 us -> 18.4 us  [call(): pl.pallas_call(kernel, out_shape=out_shapes, in_specs=[SMEM if a.ndim ==...]
  transfers between devices with their start and end apart: 45 -> 48, of which waited for: 29 -> 31; matrix products, arithmetic and copies ran while one was open for 0% -> 0% of each run, Pallas kernels for 4% -> 4%
where the time goes in v2:
time: 198 us
  starting transfers between devices  73.5 us (37%)
  waiting for transfers between devices  72.6 us (37%)
  blocking collectives  31.1 us (16%)
  Pallas kernels  18.4 us (9%)
    ppermute x48, starting transfers between devices, moved(): return lax.ppermute(block, axes, pairs)  73.5 us
    ppermute x48, waiting for transfers between devices, moved(): return lax.ppermute(block, axes, pairs)  72.6 us
    all_to_all x3, blocking collectives, traded(): return lax.all_to_all(blocks, axes, split_axis=0, concat_axis=0, tiled=True)  31.1 us
    pallas_call x18, Pallas kernels, call(): pl.pallas_call(kernel, out_shape=out_shapes, in_specs=[SMEM if a.ndim ==...  18.4 us
  transfers between devices with their start and end apart: 48, of which 31 were waited for; matrix products, arithmetic and copies ran while one was open for 0% of the time, Pallas kernels for 4%

profile of v2, /device:TPU:1, one launch (start us, length us, event | category | flops | bytes accessed | tf_op | source)
XLA Modules:
  0.0 197.9 jit_solution(10449366954579892765)
XLA Ops:
  2.0 2.6 %collective-permute-start.4 = (bf16[2,16,64,256]{3,2,1,0:T(8,128)(2,1)S(1)}, bf16[2,16,64,256]{3,2,1,0:T(8,128)(2,1)S(1)}, u32[]{:S(2)}, u32[]{:S(2)}) collective-permute-start(bf16[2,16,64,256]{3,2,1,0:T(8,128)(2,1)S(1)} %pad_maximum_fusion), channel_id=1, source_target_pairs={{0,1},{1,0},{2,3},{3,2},{4,5},{5,4},{6,7},{7,6},{8,9},{9,8},{10,11... | collective-permute-start | bytes 3145736 | tf_op jit(solution)/shard_map/ppermute | solution.py:44
  6.5 2.5 %collective-permute-start.1 = (bf16[2,32,2048]{2,1,0:T(8,128)(2,1)S(1)}, bf16[2,32,2048]{2,1,0:T(8,128)(2,1)S(1)}, u32[]{:S(2)}, u32[]{:S(2)}) collective-permute-start(bf16[2,32,2048]{2,1,0:T(8,128)(2,1)S(1)} %get-tuple-element.61), channel_id=1, source_target_pairs={{0,64},{32,96},{64,0},{96,32},{1,65},{33,97},{65,1},{97,33},{2,66}... | collective-permute-start | bytes 786440 | tf_op jit(solution)/shard_map/ppermute | solution.py:44
  9.1 3.0 %collective-permute-done.refs_1_.b_ref = bf16[2,32,2048]{2,1,0:T(8,128)(2,1)S(1)} collective-permute-done((bf16[2,32,2048]{2,1,0:T(8,128)(2,1)S(1)}, bf16[2,32,2048]{2,1,0:T(8,128)(2,1)S(1)}, u32[]{:S(2)}, u32[]{:S(2)}) %collective-permute-start) | collective-permute-done | bytes 262176 | tf_op jit(solution)/shard_map/ppermute | solution.py:44
  12.1 7.9 %collective-permute-done.1.refs_2_.c_ref = bf16[2,32,2048]{2,1,0:T(8,128)(2,1)S(1)} collective-permute-done((bf16[2,32,2048]{2,1,0:T(8,128)(2,1)S(1)}, bf16[2,32,2048]{2,1,0:T(8,128)(2,1)S(1)}, u32[]{:S(2)}, u32[]{:S(2)}) %collective-permute-start.1) | collective-permute-done | bytes 262176 | tf_op jit(solution)/shard_map/ppermute | solution.py:44
  30.8 11.9 %all_to_all.15.sums_ref = bf16[8,16,1152]{2,1,0:T(8,128)(2,1)S(1)} all-to-all(bf16[8,16,1152]{2,1,0:T(8,128)(2,1)S(1)} %add_cores_pair.1), channel_id=1, replica_groups=mesh['s'=2,'x'=4,'c'=2,'y'=4,'zh'=2,'zl'=2] {'x','zl'}, dimensions={0} | all-to-all | bytes 589824 | tf_op jit(solution)/shard_map/all_to_all | solution.py:325
  45.0 8.9 %all_to_all.16 = bf16[8,16,1024]{2,1,0:T(8,128)(2,1)S(1)} all-to-all(bf16[8,16,1024]{2,1,0:T(8,128)(2,1)S(1)} %attend_pair.1), channel_id=1, replica_groups=mesh['s'=2,'x'=4,'c'=2,'y'=4,'zh'=2,'zl'=2] {'x','zl'}, dimensions={0} | all-to-all | bytes 524288 | tf_op jit(solution)/shard_map/all_to_all | solution.py:325
  61.1 2.6 %collective-permute-start.8 = (bf16[2,256,128]{2,1,0:T(8,128)(2,1)S(1)}, bf16[2,256,128]{2,1,0:T(8,128)(2,1)S(1)}, u32[]{:S(2)}, u32[]{:S(2)}) collective-permute-start(bf16[2,256,128]{2,1,0:T(8,128)(2,1)S(1)} %get-tuple-element.71), channel_id=1, source_target_pairs={{0,8},{4,12},{8,0},{12,4},{1,9},{5,13},{9,1},{13,5},{2,10},{6,14},... | collective-permute-start | bytes 393224 | tf_op jit(solution)/shard_map/ppermute | solution.py:44
  64.4 3.1 %collective-permute-start.12 = (bf16[2,256,128]{2,1,0:T(8,128)(2,1)S(1)}, bf16[2,256,128]{2,1,0:T(8,128)(2,1)S(1)}, u32[]{:S(2)}, u32[]{:S(2)}) collective-permute-start(bf16[2,256,128]{2,1,0:T(8,128)(2,1)S(1)} %get-tuple-element.78), channel_id=1, source_target_pairs={{0,8},{4,12},{8,0},{12,4},{1,9},{5,13},{9,1},{13,5},{2,10},{6,14},... | collective-permute-start | bytes 393224 | tf_op jit(solution)/shard_map/ppermute | solution.py:44
  72.3 3.5 %collective-permute-start.16 = (bf16[256,128]{1,0:T(8,128)(2,1)S(1)}, bf16[256,128]{1,0:T(8,128)(2,1)S(1)}, u32[]{:S(2)}, u32[]{:S(2)}) collective-permute-start(bf16[256,128]{1,0:T(8,128)(2,1)S(1)} %get-tuple-element.82), channel_id=1, source_target_pairs={{0,3},{1,2},{2,1},{3,0},{4,7},{5,6},{6,5},{7,4},{8,11},{9,10},{10,... | collective-permute-start | bytes 196616 | tf_op jit(solution)/shard_map/ppermute | solution.py:44
  75.9 2.5 %collective-permute-done.13.refs_3_ = bf16[2,256,128]{2,1,0:T(8,128)(2,1)S(1)} collective-permute-done((bf16[2,256,128]{2,1,0:T(8,128)(2,1)S(1)}, bf16[2,256,128]{2,1,0:T(8,128)(2,1)S(1)}, u32[]{:S(2)}, u32[]{:S(2)}) %collective-permute-start.13) | collective-permute-done | bytes 131104 | tf_op jit(solution)/shard_map/ppermute | solution.py:44
  79.1 2.9 %collective-permute-start.15 = (bf16[256,128]{1,0:T(8,128)(2,1)S(1)}, bf16[256,128]{1,0:T(8,128)(2,1)S(1)}, u32[]{:S(2)}, u32[]{:S(2)}) collective-permute-start(bf16[256,128]{1,0:T(8,128)(2,1)S(1)} %get-tuple-element.81), channel_id=1, source_target_pairs={{0,2},{1,3},{2,0},{3,1},{4,6},{5,7},{6,4},{7,5},{8,10},{9,11},{10,... | collective-permute-start | bytes 196616 | tf_op jit(solution)/shard_map/ppermute | solution.py:44
  83.7 4.9 %collective-permute-start.17 = (bf16[256,128]{1,0:T(8,128)(2,1)S(1)}, bf16[256,128]{1,0:T(8,128)(2,1)S(1)}, u32[]{:S(2)}, u32[]{:S(2)}) collective-permute-start(bf16[256,128]{1,0:T(8,128)(2,1)S(1)} %merge_state.1.refs_5_), channel_id=1, source_target_pairs={{0,131},{1,130},{2,129},{3,128},{128,3},{129,2},{130,1},{131,0},{4... | collective-permute-start | bytes 196616 | tf_op jit(solution)/shard_map/ppermute | solution.py:44
  98.2 2.5 %collective-permute-start.21 = (bf16[4,256,128]{2,1,0:T(8,128)(2,1)S(1)}, bf16[4,256,128]{2,1,0:T(8,128)(2,1)S(1)}, u32[]{:S(2)}, u32[]{:S(2)}) collective-permute-start(bf16[4,256,128]{2,1,0:T(8,128)(2,1)S(1)} %pad_maximum_fusion.1.a_ref), channel_id=1, source_target_pairs={{0,4},{4,0},{8,12},{12,8},{1,5},{5,1},{9,13},{13,9},{2,6},{6,2},{1... | collective-permute-start | bytes 786440 | tf_op jit(solution)/shard_map/ppermute | solution.py:44
  101.0 6.2 %collective-permute-done.23.d_ref = bf16[4,256,128]{2,1,0:T(8,128)(2,1)S(1)} collective-permute-done((bf16[4,256,128]{2,1,0:T(8,128)(2,1)S(1)}, bf16[4,256,128]{2,1,0:T(8,128)(2,1)S(1)}, u32[]{:S(2)}, u32[]{:S(2)}) %collective-permute-start.23) | collective-permute-done | bytes 262176 | tf_op jit(solution)/shard_map/ppermute | solution.py:44
  109.8 6.1 %collective-permute-start.24 = (bf16[128,1152]{1,0:T(8,128)(2,1)S(1)}, bf16[128,1152]{1,0:T(8,128)(2,1)S(1)}, u32[]{:S(2)}, u32[]{:S(2)}) collective-permute-start(bf16[128,1152]{1,0:T(8,128)(2,1)S(1)} %get-tuple-element.86), channel_id=1, source_target_pairs={{0,16},{16,0},{1,17},{17,1},{2,18},{18,2},{3,19},{19,3},{4,20},{20... | collective-permute-start | bytes 884744 | tf_op jit(solution)/shard_map/ppermute | solution.py:44
  123.7 3.1 %attend.1.refs_0_ = bf16[32,1024]{1,0:T(8,128)(2,1)S(1)} custom-call(s32[6]{0:T(128)S(1)} %stack.62.place_ref, s32[32]{0:T(128)S(1)} %copy-done.5, bf16[32,1152]{1,0:T(8,128)(2,1)S(1)} %get-tuple-element.87.a_ref, bf16[32,1152]{1,0:T(8,128)(2,1)S(1)} %collective-permute-done.25.b_ref, bf16[32,1152]{1,0:T(8,128)(2,1)S(1)} %collective-permute-done.26.c_ref, ...), custom_call_target="tpu_custom_call" | custom-call | flops 1073741824 | bytes 4554904 | tf_op jit(solution)/shard_map/attend/pallas_call | solution.py:26
  126.9 2.4 %collective-permute-start.31 = (bf16[32,1024]{1,0:T(8,128)(2,1)S(1)}, bf16[32,1024]{1,0:T(8,128)(2,1)S(1)}, u32[]{:S(2)}, u32[]{:S(2)}) collective-permute-start(bf16[32,1024]{1,0:T(8,128)(2,1)S(1)} %attend.1.refs_0_), channel_id=1, source_target_pairs={{0,96},{32,64},{64,32},{96,0},{1,97},{33,65},{65,33},{97,1},{2,98}... | collective-permute-start | bytes 196616 | tf_op jit(solution)/shard_map/ppermute | solution.py:44
  131.3 2.7 %collective-permute-done.30.refs_2_ = bf16[32,1024]{1,0:T(8,128)(2,1)S(1)} collective-permute-done((bf16[32,1024]{1,0:T(8,128)(2,1)S(1)}, bf16[32,1024]{1,0:T(8,128)(2,1)S(1)}, u32[]{:S(2)}, u32[]{:S(2)}) %collective-permute-start.30) | collective-permute-done | bytes 65568 | tf_op jit(solution)/shard_map/ppermute | solution.py:44
  134.0 3.2 %collective-permute-start.32 = (bf16[4,32,1024]{2,1,0:T(8,128)(2,1)S(1)}, bf16[4,32,1024]{2,1,0:T(8,128)(2,1)S(1)}, u32[]{:S(2)}, u32[]{:S(2)}) collective-permute-start(bf16[4,32,1024]{2,1,0:T(8,128)(2,1)S(1)} %pick.3.near_ref), channel_id=1, source_target_pairs={{0,16},{16,0},{1,17},{17,1},{2,18},{18,2},{3,19},{19,3},{4,20},{20... | collective-permute-start | bytes 786440 | tf_op jit(solution)/shard_map/ppermute | solution.py:44
  153.9 2.4 %collective-permute-done.38.refs_3_ = bf16[2,256,128]{2,1,0:T(8,128)(2,1)S(1)} collective-permute-done((bf16[2,256,128]{2,1,0:T(8,128)(2,1)S(1)}, bf16[2,256,128]{2,1,0:T(8,128)(2,1)S(1)}, u32[]{:S(2)}, u32[]{:S(2)}) %collective-permute-start.38) | collective-permute-done | bytes 131104 | tf_op jit(solution)/shard_map/ppermute | solution.py:44
  162.6 10.3 %all_to_all.17 = bf16[8,32,128]{2,1,0:T(8,128)(2,1)S(1)} all-to-all(bf16[8,32,128]{2,1,0:T(8,128)(2,1)S(1)} %merge_last.1), channel_id=1, replica_groups=mesh['s'=2,'x'=4,'c'=2,'y'=4,'zh'=2,'zl'=2] {'x','c'}, dimensions={0} | all-to-all | bytes 131072 | tf_op jit(solution)/shard_map/all_to_all | solution.py:325
  177.8 3.6 %collective-permute-done.43 = bf16[8,32,128]{2,1,0:T(8,128)(2,1)S(1)} collective-permute-done((bf16[8,32,128]{2,1,0:T(8,128)(2,1)S(1)}, bf16[8,32,128]{2,1,0:T(8,128)(2,1)S(1)}, u32[]{:S(2)}, u32[]{:S(2)}) %collective-permute-start.43) | collective-permute-done | bytes 65568 | tf_op jit(solution)/shard_map/ppermute | solution.py:44
  181.5 2.4 %collective-permute-start.47 = (bf16[4,8,32,128]{3,2,1,0:T(8,128)(2,1)S(1)}, bf16[4,8,32,128]{3,2,1,0:T(8,128)(2,1)S(1)}, u32[]{:S(2)}, u32[]{:S(2)}) collective-permute-start(bf16[4,8,32,128]{3,2,1,0:T(8,128)(2,1)S(1)} %pad_maximum_fusion.2.refs_0_), channel_id=1, source_target_pairs={{0,12},{4,8},{8,4},{12,0},{1,13},{5,9},{9,5},{13,1},{2,14},{6,10},... | collective-permute-start | bytes 786440 | tf_op jit(solution)/shard_map/ppermute | solution.py:44
  184.8 10.9 %collective-permute-done.47.refs_3_ = bf16[4,8,32,128]{3,2,1,0:T(8,128)(2,1)S(1)} collective-permute-done((bf16[4,8,32,128]{3,2,1,0:T(8,128)(2,1)S(1)}, bf16[4,8,32,128]{3,2,1,0:T(8,128)(2,1)S(1)}, u32[]{:S(2)}, u32[]{:S(2)}) %collective-permute-start.47) | collective-permute-done | bytes 262176 | tf_op jit(solution)/shard_map/ppermute | solution.py:44
  (110 shorter events, 85.6 us)
Async XLA Ops:
  2.0 26.5 %collective-permute-start.4 = (bf16[2,16,64,256]{3,2,1,0:T(8,128)(2,1)S(1)}, bf16[2,16,64,256]{3,2,1,0:T(8,128)(2,1)S(1)}, u32[]{:S(2)}, u32[]{:S(2)}) collective-permute-start(bf16[2,16,64,256]{3,2,1,0:T(8,128)(2,1)S(1)} %pad_maximum_fusion), channel_id=1, source_target_pairs={{0,1},{1,0},{2,3},{3,2},{4,5},{5,4},{6,7},{7,6},{8,9},{9,8},{10,11... | collective-permute-start | bytes 3145736 | tf_op jit(solution)/shard_map/ppermute | solution.py:44
  6.5 13.5 %collective-permute-start.1 = (bf16[2,32,2048]{2,1,0:T(8,128)(2,1)S(1)}, bf16[2,32,2048]{2,1,0:T(8,128)(2,1)S(1)}, u32[]{:S(2)}, u32[]{:S(2)}) collective-permute-start(bf16[2,32,2048]{2,1,0:T(8,128)(2,1)S(1)} %get-tuple-element.61), channel_id=1, source_target_pairs={{0,64},{32,96},{64,0},{96,32},{1,65},{33,97},{65,1},{97,33},{2,66}... | collective-permute-start | bytes 786440 | tf_op jit(solution)/shard_map/ppermute | solution.py:44
  9.0 13.4 %collective-permute-start.2 = (bf16[2,32,2048]{2,1,0:T(8,128)(2,1)S(1)}, bf16[2,32,2048]{2,1,0:T(8,128)(2,1)S(1)}, u32[]{:S(2)}, u32[]{:S(2)}) collective-permute-start(bf16[2,32,2048]{2,1,0:T(8,128)(2,1)S(1)} %get-tuple-element.62), channel_id=1, source_target_pairs={{0,96},{32,64},{64,32},{96,0},{1,97},{33,65},{65,33},{97,1},{2,98}... | collective-permute-start | bytes 786440 | tf_op jit(solution)/shard_map/ppermute | solution.py:44
  56.3 19.5 %collective-permute-start.10 = (bf16[16,64,256]{2,1,0:T(8,128)(2,1)S(1)}, bf16[16,64,256]{2,1,0:T(8,128)(2,1)S(1)}, u32[]{:S(2)}, u32[]{:S(2)}) collective-permute-start(bf16[16,64,256]{2,1,0:T(8,128)(2,1)S(1)} %get-tuple-element.75.key_ref), channel_id=1, source_target_pairs={{0,1},{1,0},{2,3},{3,2},{4,5},{5,4},{6,7},{7,6},{8,9},{9,8},{10,11... | collective-permute-start | bytes 1572872 | tf_op jit(solution)/shard_map/ppermute | solution.py:44
  61.1 8.7 %collective-permute-start.8 = (bf16[2,256,128]{2,1,0:T(8,128)(2,1)S(1)}, bf16[2,256,128]{2,1,0:T(8,128)(2,1)S(1)}, u32[]{:S(2)}, u32[]{:S(2)}) collective-permute-start(bf16[2,256,128]{2,1,0:T(8,128)(2,1)S(1)} %get-tuple-element.71), channel_id=1, source_target_pairs={{0,8},{4,12},{8,0},{12,4},{1,9},{5,13},{9,1},{13,5},{2,10},{6,14},... | collective-permute-start | bytes 393224 | tf_op jit(solution)/shard_map/ppermute | solution.py:44
  63.7 8.6 %collective-permute-start.9 = (bf16[2,256,128]{2,1,0:T(8,128)(2,1)S(1)}, bf16[2,256,128]{2,1,0:T(8,128)(2,1)S(1)}, u32[]{:S(2)}, u32[]{:S(2)}) collective-permute-start(bf16[2,256,128]{2,1,0:T(8,128)(2,1)S(1)} %get-tuple-element.72), channel_id=1, source_target_pairs={{0,12},{4,8},{8,4},{12,0},{1,13},{5,9},{9,5},{13,1},{2,14},{6,10},... | collective-permute-start | bytes 393224 | tf_op jit(solution)/shard_map/ppermute | solution.py:44
  63.7 12.2 %collective-permute-start.11 = (bf16[2,256,128]{2,1,0:T(8,128)(2,1)S(1)}, bf16[2,256,128]{2,1,0:T(8,128)(2,1)S(1)}, u32[]{:S(2)}, u32[]{:S(2)}) collective-permute-start(bf16[2,256,128]{2,1,0:T(8,128)(2,1)S(1)} %get-tuple-element.77), channel_id=1, source_target_pairs={{0,4},{4,0},{8,12},{12,8},{1,5},{5,1},{9,13},{13,9},{2,6},{6,2},{1... | collective-permute-start | bytes 393224 | tf_op jit(solution)/shard_map/ppermute | solution.py:44
  64.4 11.4 %collective-permute-start.12 = (bf16[2,256,128]{2,1,0:T(8,128)(2,1)S(1)}, bf16[2,256,128]{2,1,0:T(8,128)(2,1)S(1)}, u32[]{:S(2)}, u32[]{:S(2)}) collective-permute-start(bf16[2,256,128]{2,1,0:T(8,128)(2,1)S(1)} %get-tuple-element.78), channel_id=1, source_target_pairs={{0,8},{4,12},{8,0},{12,4},{1,9},{5,13},{9,1},{13,5},{2,10},{6,14},... | collective-permute-start | bytes 393224 | tf_op jit(solution)/shard_map/ppermute | solution.py:44
  69.8 8.6 %collective-permute-start.13 = (bf16[2,256,128]{2,1,0:T(8,128)(2,1)S(1)}, bf16[2,256,128]{2,1,0:T(8,128)(2,1)S(1)}, u32[]{:S(2)}, u32[]{:S(2)}) collective-permute-start(bf16[2,256,128]{2,1,0:T(8,128)(2,1)S(1)} %get-tuple-element.79), channel_id=1, source_target_pairs={{0,12},{4,8},{8,4},{12,0},{1,13},{5,9},{9,5},{13,1},{2,14},{6,10},... | collective-permute-start | bytes 393224 | tf_op jit(solution)/shard_map/ppermute | solution.py:44
  72.3 9.7 %collective-permute-start.16 = (bf16[256,128]{1,0:T(8,128)(2,1)S(1)}, bf16[256,128]{1,0:T(8,128)(2,1)S(1)}, u32[]{:S(2)}, u32[]{:S(2)}) collective-permute-start(bf16[256,128]{1,0:T(8,128)(2,1)S(1)} %get-tuple-element.82), channel_id=1, source_target_pairs={{0,3},{1,2},{2,1},{3,0},{4,7},{5,6},{6,5},{7,4},{8,11},{9,10},{10,... | collective-permute-start | bytes 196616 | tf_op jit(solution)/shard_map/ppermute | solution.py:44
  97.3 9.9 %collective-permute-start.23 = (bf16[4,256,128]{2,1,0:T(8,128)(2,1)S(1)}, bf16[4,256,128]{2,1,0:T(8,128)(2,1)S(1)}, u32[]{:S(2)}, u32[]{:S(2)}) collective-permute-start(bf16[4,256,128]{2,1,0:T(8,128)(2,1)S(1)} %pad_maximum_fusion.1.a_ref), channel_id=1, source_target_pairs={{0,12},{4,8},{8,4},{12,0},{1,13},{5,9},{9,5},{13,1},{2,14},{6,10},... | collective-permute-start | bytes 786440 | tf_op jit(solution)/shard_map/ppermute | solution.py:44
  97.8 9.5 %collective-permute-start.22 = (bf16[4,256,128]{2,1,0:T(8,128)(2,1)S(1)}, bf16[4,256,128]{2,1,0:T(8,128)(2,1)S(1)}, u32[]{:S(2)}, u32[]{:S(2)}) collective-permute-start(bf16[4,256,128]{2,1,0:T(8,128)(2,1)S(1)} %pad_maximum_fusion.1.a_ref), channel_id=1, source_target_pairs={{0,8},{4,12},{8,0},{12,4},{1,9},{5,13},{9,1},{13,5},{2,10},{6,14},... | collective-permute-start | bytes 786440 | tf_op jit(solution)/shard_map/ppermute | solution.py:44
  98.2 9.5 %collective-permute-start.21 = (bf16[4,256,128]{2,1,0:T(8,128)(2,1)S(1)}, bf16[4,256,128]{2,1,0:T(8,128)(2,1)S(1)}, u32[]{:S(2)}, u32[]{:S(2)}) collective-permute-start(bf16[4,256,128]{2,1,0:T(8,128)(2,1)S(1)} %pad_maximum_fusion.1.a_ref), channel_id=1, source_target_pairs={{0,4},{4,0},{8,12},{12,8},{1,5},{5,1},{9,13},{13,9},{2,6},{6,2},{1... | collective-permute-start | bytes 786440 | tf_op jit(solution)/shard_map/ppermute | solution.py:44
  100.7 20.5 %collective-permute-start.28 = (bf16[16,64,256]{2,1,0:T(8,128)(2,1)S(1)}, bf16[16,64,256]{2,1,0:T(8,128)(2,1)S(1)}, u32[]{:S(2)}, u32[]{:S(2)}) collective-permute-start(bf16[16,64,256]{2,1,0:T(8,128)(2,1)S(1)} %get-tuple-element.92.value_ref), channel_id=1, source_target_pairs={{0,1},{1,0},{2,3},{3,2},{4,5},{5,4},{6,7},{7,6},{8,9},{9,8},{10,11... | collective-permute-start | bytes 1572872 | tf_op jit(solution)/shard_map/ppermute | solution.py:44
  109.8 7.3 %collective-permute-start.24 = (bf16[128,1152]{1,0:T(8,128)(2,1)S(1)}, bf16[128,1152]{1,0:T(8,128)(2,1)S(1)}, u32[]{:S(2)}, u32[]{:S(2)}) collective-permute-start(bf16[128,1152]{1,0:T(8,128)(2,1)S(1)} %get-tuple-element.86), channel_id=1, source_target_pairs={{0,16},{16,0},{1,17},{17,1},{2,18},{18,2},{3,19},{19,3},{4,20},{20... | collective-permute-start | bytes 884744 | tf_op jit(solution)/shard_map/ppermute | solution.py:44
  140.7 7.7 %collective-permute-start.34 = (bf16[2,256,128]{2,1,0:T(8,128)(2,1)S(1)}, bf16[2,256,128]{2,1,0:T(8,128)(2,1)S(1)}, u32[]{:S(2)}, u32[]{:S(2)}) collective-permute-start(bf16[2,256,128]{2,1,0:T(8,128)(2,1)S(1)} %get-tuple-element.95), channel_id=1, source_target_pairs={{0,8},{4,12},{8,0},{12,4},{1,9},{5,13},{9,1},{13,5},{2,10},{6,14},... | collective-permute-start | bytes 393224 | tf_op jit(solution)/shard_map/ppermute | solution.py:44
  142.2 8.6 %collective-permute-start.35 = (bf16[2,256,128]{2,1,0:T(8,128)(2,1)S(1)}, bf16[2,256,128]{2,1,0:T(8,128)(2,1)S(1)}, u32[]{:S(2)}, u32[]{:S(2)}) collective-permute-start(bf16[2,256,128]{2,1,0:T(8,128)(2,1)S(1)} %get-tuple-element.96), channel_id=1, source_target_pairs={{0,12},{4,8},{8,4},{12,0},{1,13},{5,9},{9,5},{13,1},{2,14},{6,10},... | collective-permute-start | bytes 393224 | tf_op jit(solution)/shard_map/ppermute | solution.py:44
  144.5 8.0 %collective-permute-start.36 = (bf16[2,256,128]{2,1,0:T(8,128)(2,1)S(1)}, bf16[2,256,128]{2,1,0:T(8,128)(2,1)S(1)}, u32[]{:S(2)}, u32[]{:S(2)}) collective-permute-start(bf16[2,256,128]{2,1,0:T(8,128)(2,1)S(1)} %get-tuple-element.99), channel_id=1, source_target_pairs={{0,4},{4,0},{8,12},{12,8},{1,5},{5,1},{9,13},{13,9},{2,6},{6,2},{1... | collective-permute-start | bytes 393224 | tf_op jit(solution)/shard_map/ppermute | solution.py:44
  144.5 9.4 %collective-permute-start.37 = (bf16[2,256,128]{2,1,0:T(8,128)(2,1)S(1)}, bf16[2,256,128]{2,1,0:T(8,128)(2,1)S(1)}, u32[]{:S(2)}, u32[]{:S(2)}) collective-permute-start(bf16[2,256,128]{2,1,0:T(8,128)(2,1)S(1)} %get-tuple-element.100), channel_id=1, source_target_pairs={{0,8},{4,12},{8,0},{12,4},{1,9},{5,13},{9,1},{13,5},{2,10},{6,14},... | collective-permute-start | bytes 393224 | tf_op jit(solution)/shard_map/ppermute | solution.py:44
  146.0 10.3 %collective-permute-start.38 = (bf16[2,256,128]{2,1,0:T(8,128)(2,1)S(1)}, bf16[2,256,128]{2,1,0:T(8,128)(2,1)S(1)}, u32[]{:S(2)}, u32[]{:S(2)}) collective-permute-start(bf16[2,256,128]{2,1,0:T(8,128)(2,1)S(1)} %get-tuple-element.101), channel_id=1, source_target_pairs={{0,12},{4,8},{8,4},{12,0},{1,13},{5,9},{9,5},{13,1},{2,14},{6,10},... | collective-permute-start | bytes 393224 | tf_op jit(solution)/shard_map/ppermute | solution.py:44
  150.8 7.6 %collective-permute-start.41 = (bf16[256,128]{1,0:T(8,128)(2,1)S(1)}, bf16[256,128]{1,0:T(8,128)(2,1)S(1)}, u32[]{:S(2)}, u32[]{:S(2)}) collective-permute-start(bf16[256,128]{1,0:T(8,128)(2,1)S(1)} %get-tuple-element.104), channel_id=1, source_target_pairs={{0,3},{1,2},{2,1},{3,0},{4,7},{5,6},{6,5},{7,4},{8,11},{9,10},{10,... | collective-permute-start | bytes 196616 | tf_op jit(solution)/shard_map/ppermute | solution.py:44
  181.5 14.2 %collective-permute-start.47 = (bf16[4,8,32,128]{3,2,1,0:T(8,128)(2,1)S(1)}, bf16[4,8,32,128]{3,2,1,0:T(8,128)(2,1)S(1)}, u32[]{:S(2)}, u32[]{:S(2)}) collective-permute-start(bf16[4,8,32,128]{3,2,1,0:T(8,128)(2,1)S(1)} %pad_maximum_fusion.2.refs_0_), channel_id=1, source_target_pairs={{0,12},{4,8},{8,4},{12,0},{1,13},{5,9},{9,5},{13,1},{2,14},{6,10},... | collective-permute-start | bytes 786440 | tf_op jit(solution)/shard_map/ppermute | solution.py:44
  183.9 11.8 %collective-permute-start.46 = (bf16[4,8,32,128]{3,2,1,0:T(8,128)(2,1)S(1)}, bf16[4,8,32,128]{3,2,1,0:T(8,128)(2,1)S(1)}, u32[]{:S(2)}, u32[]{:S(2)}) collective-permute-start(bf16[4,8,32,128]{3,2,1,0:T(8,128)(2,1)S(1)} %pad_maximum_fusion.2.refs_0_), channel_id=1, source_target_pairs={{0,8},{4,12},{8,0},{12,4},{1,9},{5,13},{9,1},{13,5},{2,10},{6,14},... | collective-permute-start | bytes 786440 | tf_op jit(solution)/shard_map/ppermute | solution.py:44
  183.9 12.1 %collective-permute-start.45 = (bf16[4,8,32,128]{3,2,1,0:T(8,128)(2,1)S(1)}, bf16[4,8,32,128]{3,2,1,0:T(8,128)(2,1)S(1)}, u32[]{:S(2)}, u32[]{:S(2)}) collective-permute-start(bf16[4,8,32,128]{3,2,1,0:T(8,128)(2,1)S(1)} %pad_maximum_fusion.2.refs_0_), channel_id=1, source_target_pairs={{0,4},{4,0},{8,12},{12,8},{1,5},{5,1},{9,13},{13,9},{2,6},{6,2},{1... | collective-permute-start | bytes 786440 | tf_op jit(solution)/shard_map/ppermute | solution.py:44
  (30 other events, 322.7 us)
